TPU v7x, 256 devices: a whole 4x4x8 slice. The times are simulated.
256 devices in a mesh: lat: 32 (over z, x_hi, core), lon: 8 (over x_lo, y).
Axes of the slice: x: 4 (x_hi: 2, x_lo: 2; x = x_hi * 2 + x_lo), y: 4, z: 8, core: 2. Of those that a mesh axis runs over, the one named last changes fastest.
Arguments:
- input_field: bfloat16 [128, 2048, 256], P('lat', 'lon'), may hold values from -6 to 6
- grad_out: bfloat16 [128, 2048, 256], P('lat', 'lon'), may hold values from -6 to 6
- weight: bfloat16 [2304, 256], replicated, may hold values from -0.375 to 0.375
- filt: bfloat16 [9, 128, 3, 33], P(None, 'lat'), may hold values from -0.875 to 0.875
- zonal_weight: bfloat16 [9, 128, 3, 2048], P(None, 'lat'), may hold values from -0.078125 to 0.078125
- widths: int32 [128], P('lat'), may hold values from 1 to 16, as said below
- offsets: int32 [128], P('lat'), may hold values from -2 to 0
- polar_rows: int32 [4], replicated, may hold values from 0 to 127, as said below
Outputs:
- input_grad: bfloat16 [128, 2048, 256], P('lat', 'lon')
- weight_grad: float32 [2304, 256], P('lat')
Inputs may be any that keep to these rules, and one draw needn't show every extreme that they name: `widths`: every row's half-width is between 1 and 16; the first and last rows have 16. `polar_rows`: four distinct rows: entry 0 is the first row and entry 1 another of the first 4 rows; entry 2 is the last row and entry 3 another of the last 4 rows.
All inputs are finite; a program needn't handle non-finite values.
Results may differ from a plain program's by a relative error of at most 0.0075.
Values may be sent and summed in bfloat16 or wider, within the bound.
A program may use at most 256 MiB of HBM per device.

v0:
```python
import functools
import math

import jax
import jax.numpy as jnp
from jax import lax
from jax.experimental import pallas as pl
from jax.experimental.pallas import tpu as pltpu
from jax.sharding import PartitionSpec as P

MESH = pl.DeviceIdType.MESH
F32 = jnp.float32
BF16 = jnp.bfloat16
ROWS = 4
LONS = 256
C = 256
K = 9
REACH = 16
JB = 64
WIN = JB + 2 * REACH
CANDS = 5
DEPTH = 512
N_LAT = 32
N_LON = 8
N_P = 16
GROUPS = ((0, 3), (3, 6), (6, 9))
FACTOR = 1.0 / math.sqrt(128 * 2048)


def dot(a, b, ca=1, cb=0):
    return lax.dot_general(a, b, (((ca,), (cb,)), ((), ())), preferred_element_type=F32)


def kernel(
    g_hbm, x_hbm, w_hbm, v_ref, y_ref, polar_ref,
    ig_hbm, wg_ref,
    gx, xv, xt, wv, wt, vh, yh, vf, tt, hh, yy, ztf, zst, gs_own, gs_buf, gsel,
    wown, wsnd, cx, s1, rb, s2, pr, s3, fin, igv,
    loc_sem, halo_send, halo_recv, vsend, vrecv, ysend, yrecv, gs_send, gs_sem,
    cs_send, cs_recv, ls_send, ls_recv, ps_send, ps_recv, fs_send, fs_recv, out_sem,
):
    lat = lax.axis_index("lat")
    lon = lax.axis_index("lon")
    core = lax.rem(lat, 2)
    p = lax.div(lat, 2)
    twin = lat + 1 - 2 * core

    def lon_at(step):
        return lax.rem(lon + step, N_LON)

    def remote(src, dst, send, recv, to_lat, to_lon):
        return pltpu.make_async_remote_copy(
            src_ref=src, dst_ref=dst, send_sem=send, recv_sem=recv,
            device_id={"lat": to_lat, "lon": to_lon}, device_id_type=MESH,
        )

    g_copy = pltpu.make_async_copy(g_hbm, gx.at[pl.ds(2, ROWS), pl.ds(REACH, LONS)], loc_sem.at[0])
    x_copy = pltpu.make_async_copy(x_hbm, xv, loc_sem.at[1])
    w_copy = pltpu.make_async_copy(w_hbm, wv, loc_sem.at[2])
    g_copy.start()
    x_copy.start()
    w_copy.start()

    barrier = pltpu.get_barrier_semaphore()

    def greet(to_lat, to_lon):
        pl.semaphore_signal(barrier, inc=1, device_id={"lat": to_lat, "lon": to_lon}, device_id_type=MESH)

    outer = lat - 1 + 2 * core
    has_outer = (outer >= 0) & (outer < N_LAT)

    @pl.when(has_outer)
    def _():
        for step in (0, 1, N_LON - 1):
            greet(outer, lon_at(step))

    for step in range(1, N_LON):
        greet(lat, lon_at(step))
    for step in range(N_LON):
        greet(twin, lon_at(step))
    for step in range(1, N_P):
        greet(2 * lax.rem(p + step, N_P) + core, lon)
    pl.semaphore_wait(barrier, 2 * N_LON + N_P - 2 + 3 * has_outer.astype(jnp.int32))

    up, down = lat - 1, lat + 1
    has_up, has_down = lat > 0, lat < N_LAT - 1
    left, right = lon_at(N_LON - 1), lon_at(1)
    rows_of = {-1: (0, 2, 6), 0: (0, ROWS, 2), 1: (2, 2, 0)}
    cols_of = {-1: (0, REACH, REACH + LONS), 0: (0, LONS, REACH), 1: (LONS - REACH, REACH, 0)}
    moves = [(1, 0), (-1, 0), (0, 1), (0, -1), (1, 1), (1, -1), (-1, 1), (-1, -1)]

    def halo(index):
        dlat, dlon = moves[index]
        r0, rn, r_to = rows_of[dlat]
        c0, cn, c_to = cols_of[dlon]
        return remote(
            g_hbm.at[pl.ds(r0, rn), pl.ds(c0, cn)],
            gx.at[pl.ds(r_to, rn), pl.ds(c_to, cn)],
            halo_send.at[index], halo_recv.at[index],
            lat + dlat, lon_at(dlon % N_LON),
        )

    def can_send(index):
        dlat = moves[index][0]
        return has_down if dlat == 1 else has_up

    def can_recv(index):
        dlat = moves[index][0]
        return has_up if dlat == 1 else has_down

    def v_halo(side):
        src = v_ref.at[pl.ds(6, 2)] if side == 0 else v_ref.at[pl.ds(0, 2)]
        return remote(src, vh.at[side], vsend.at[side], vrecv.at[side], down if side == 0 else up, lon)

    for side in range(2):
        @pl.when(has_down if side == 0 else has_up)
        def _():
            v_halo(side).start()

    for index in range(8):
        if moves[index][0] == 0:
            halo(index).start()
        else:
            @pl.when(can_send(index))
            def _():
                halo(index).start()

    north, south = lat == 0, lat == N_LAT - 1
    polar_dev = north | south
    affected = polar_dev | (lat == 1) | (lat == N_LAT - 2)

    def y_halo(first):
        return remote(y_ref.at[pl.ds(first, 2)], yh, ysend, yrecv, twin, lon)

    @pl.when(north)
    def _():
        y_halo(6).start()

    @pl.when(south)
    def _():
        y_halo(0).start()

    g_copy.wait()

    def gs_copy(dc, step):
        return remote(gs_own, gs_buf.at[lon], gs_send.at[dc, step], gs_sem, twin if dc else lat, lon_at(step))

    @pl.when(polar_dev)
    def _():
        gs_own[...] = jnp.zeros_like(gs_own)
        for i in range(ROWS):
            gs_own[pl.ds(i, 1), :] = jnp.sum(
                gx[2 + i, pl.ds(REACH, LONS), :].astype(F32), axis=0, keepdims=True
            )
        for dc in range(2):
            for step in range(N_LON):
                if dc or step:
                    gs_copy(dc, step).start()
        pltpu.make_async_copy(gs_own, gs_buf.at[lon], gs_sem).start()

    @pl.when(lat == 0)
    def _():
        gx[pl.ds(0, 2)] = jnp.zeros((2,) + gx.shape[1:], BF16)
        vh[0] = jnp.zeros(vh.shape[1:], BF16)

    @pl.when(lat == N_LAT - 1)
    def _():
        gx[pl.ds(6, 2)] = jnp.zeros((2,) + gx.shape[1:], BF16)
        vh[1] = jnp.zeros(vh.shape[1:], BF16)

    x_copy.wait()
    for i in range(ROWS):
        xt[:, pl.ds(i * LONS, LONS)] = xv[i].T
    w_copy.wait()

    def turn(k, carry):
        at = pl.ds(pl.multiple_of(k * C, C), C)
        wt[at, :] = wv[at, :].T
        return carry

    lax.fori_loop(0, K, turn, 0)

    for side in range(2):
        @pl.when(has_up if side == 0 else has_down)
        def _():
            v_halo(side).wait_recv()
    for i2 in range(ROWS):
        vf[pl.ds(16 * i2, 16), :] = v_ref[2 + i2].astype(F32) + vh[i2 // 2, i2 % 2].astype(F32)

    def band(index, carry):
        i2, k = lax.div(index, K), lax.rem(index, K)
        row = jnp.broadcast_to(vf[pl.ds(16 * i2 + k, 1), :], (JB, DEPTH))
        rolled = pltpu.roll(row, 0, 1, stride=1, stride_axis=0)
        tt[i2, pl.ds(pl.multiple_of(k * JB, JB), JB), :] = rolled.astype(BF16)
        return carry

    lax.fori_loop(0, ROWS * K, band, 0)

    for i2 in range(ROWS):
        yy[i2] = y_ref[2 + i2]

    @pl.when(lat == 1)
    def _():
        y_halo(6).wait_recv()
        yy[pl.ds(0, 2)] = yh[...]

    @pl.when(lat == N_LAT - 2)
    def _():
        y_halo(0).wait_recv()
        yy[pl.ds(2, 2)] = yh[...]

    circle = jnp.zeros((C, 32), F32)
    for i2 in range(ROWS):
        circle = circle + dot(xt[:, pl.ds(i2 * LONS, LONS)], yy[i2], 1, 1)
    zst[...] = circle * FACTOR

    @pl.when(jnp.logical_not(affected))
    def _():
        gsel[...] = jnp.zeros_like(gsel)

    @pl.when(affected)
    def _():
        pltpu.make_async_copy(gs_buf, gs_buf, gs_sem).wait()
        total = gs_buf[0]
        for step in range(1, N_LON):
            total = total + gs_buf[step]
        pole = lax.div(lat, N_LAT // 2)
        gsel[...] = jnp.zeros_like(gsel)
        for q in range(2):
            mine = polar_ref[2 * pole + q] - pole * (N_LAT - 1) * ROWS
            picked = jnp.zeros((1, C), F32)
            for i in range(ROWS):
                picked = picked + total[i:i + 1] * (mine == i).astype(F32)
            gsel[pl.ds(q, 1), :] = picked

    circle_sum = gsel[...]
    high = circle_sum.astype(BF16)
    low = (circle_sum - high.astype(F32)).astype(BF16)
    parts = jnp.concatenate([high.astype(F32), low.astype(F32)], axis=0).astype(BF16)
    ztf[...] = jnp.zeros_like(ztf)
    for k in range(K):
        mixed = dot(parts, wt[pl.ds(k * C, C), :])
        mixed = mixed[:8] + mixed[8:]
        for q in range(2):
            ztf[pl.ds(16 * q + k, 1), :] = mixed[q:q + 1]

    for index in range(8):
        if moves[index][0] == 0:
            halo(index).wait_recv()
        else:
            @pl.when(can_recv(index))
            def _():
                halo(index).wait_recv()

    def spread(index, carry):
        i2, jb = lax.div(index, LONS // JB), lax.rem(index, LONS // JB)
        at = pl.ds(pl.multiple_of(jb * JB, JB), WIN)
        windows = [gx[i2 + n, at, :] for n in range(CANDS)]
        windows.append(jnp.zeros((DEPTH - CANDS * WIN, C), BF16))
        moved = dot(tt[i2], jnp.concatenate(windows, axis=0)).astype(BF16)
        rows = pl.ds(pl.multiple_of(index * JB, JB), JB)
        for k in range(K):
            hh[rows, pl.ds(k * C, C)] = moved[k * JB:(k + 1) * JB]
        return carry

    lax.fori_loop(0, ROWS * LONS // JB, spread, 0)

    def twin_copy(group):
        k0, k1 = GROUPS[group]
        at = pl.ds(k0, k1 - k0)
        return remote(wsnd.at[at], cx.at[at], cs_send.at[group], cs_recv.at[group], twin, lon)

    def mix(group):
        for k in range(*GROUPS[group]):
            share = dot(xt[...], hh[:, pl.ds(k * C, C)]) * FACTOR
            for q in range(2):
                share = share + zst[:, 16 * q + k:16 * q + k + 1] * gsel[q:q + 1, :]
            first, second = share[:, :128], share[:, 128:]
            wown[k] = jnp.where(core == 0, first, second)
            wsnd[k] = jnp.where(core == 0, second, first).astype(BF16)
        twin_copy(group).start()

    def lon_copy(group, step):
        k0, k1 = GROUPS[group]
        to = lon_at(step)
        at = pl.ds(k0, k1 - k0)
        src = s1.at[at, pl.ds(pl.multiple_of(32 * to, 32), 32)]
        return remote(src, rb.at[lon, at], ls_send.at[group, step], ls_recv.at[group], lat, to)

    def over_lon(group):
        k0, k1 = GROUPS[group]
        at = pl.ds(k0, k1 - k0)
        twin_copy(group).wait_recv()
        for k in range(k0, k1):
            s1[k] = (wown[k] + cx[k].astype(F32)).astype(BF16)
        for step in range(1, N_LON):
            lon_copy(group, step).start()
        own = s1.at[at, pl.ds(pl.multiple_of(32 * lon, 32), 32)]
        pltpu.make_async_copy(own, rb.at[lon, at], ls_recv.at[group]).start()

    def granule(k, b):
        owner = lax.div(16 * k + 2 * lon + b, 9)
        copy = remote(
            s2.at[k, b], pr.at[b, p], ps_send.at[k, b], ps_recv.at[b], 2 * owner + core, lon
        )
        return owner, copy

    def over_lat(group):
        k0, k1 = GROUPS[group]
        slab = rb.at[:, pl.ds(k0, k1 - k0)]
        pltpu.make_async_copy(slab, slab, ls_recv.at[group]).wait()
        for k in range(k0, k1):
            total = rb[0, k].astype(F32)
            for step in range(1, N_LON):
                total = total + rb[step, k].astype(F32)
            total = total.astype(BF16)
            for b in range(2):
                s2[k, b] = total[16 * b:16 * b + 16]
        for k in range(k0, k1):
            for b in range(2):
                owner, copy = granule(k, b)

                @pl.when(owner != p)
                def _():
                    copy.start()

                @pl.when(owner == p)
                def _():
                    pltpu.make_async_copy(s2.at[k, b], pr.at[b, p], ps_recv.at[b]).start()

    def place(b):
        k = lax.div(9 * p - 2 * lon - b + 15, 16)
        e = 16 * k + 2 * lon + b - 9 * p
        return e, e < 9

    def final_copy(b, e, dc, step):
        at = pl.ds(pl.multiple_of(16 * e, 16), 16)
        return remote(
            s3.at[b], fin.at[core, at], fs_send.at[b, dc, step], fs_recv, twin if dc else lat, lon_at(step)
        )

    def needed(e, to_core):
        return ((to_core == 0) & (e <= 4)) | ((to_core == 1) & (e >= 4))

    def spread_out():
        for b in range(2):
            e, valid = place(b)

            @pl.when(valid)
            def _():
                pltpu.make_async_copy(pr.at[b], pr.at[b], ps_recv.at[b]).wait()
                total = pr[b, 0].astype(F32)
                for step in range(1, N_P):
                    total = total + pr[b, step].astype(F32)
                s3[b] = total

            for dc in range(2):
                @pl.when(valid & needed(e, 1 - core if dc else core))
                def _():
                    for step in range(N_LON):
                        if dc or step:
                            final_copy(b, e, dc, step).start()
                        else:
                            at = pl.ds(pl.multiple_of(16 * e, 16), 16)
                            pltpu.make_async_copy(s3.at[b], fin.at[core, at], fs_recv).start()

    def ig_copy(i2):
        return pltpu.make_async_copy(igv.at[i2], ig_hbm.at[i2], out_sem.at[i2])

    circle_total = ztf[...]
    z_high = circle_total.astype(BF16)
    z_low = (circle_total - z_high.astype(F32)).astype(BF16)
    z_parts = jnp.concatenate([z_high, z_low], axis=0)

    def pull(i2):
        grad = dot(hh[pl.ds(i2 * LONS, LONS), :], wt[...])
        twice = jnp.concatenate([yy[i2], yy[i2]], axis=0)
        igv[i2] = (grad + dot(twice, z_parts, 0, 0)).astype(BF16)
        ig_copy(i2).start()

    mix(0)
    mix(1)
    over_lon(0)
    mix(2)
    over_lon(1)
    over_lat(0)
    pull(0)
    over_lon(2)
    over_lat(1)
    pull(1)
    over_lat(2)
    pull(2)
    spread_out()
    pull(3)
    some = fin.at[:, pl.ds(0, 80)]
    pltpu.make_async_copy(some, some, fs_recv).wait()
    rows = pl.ds(pl.multiple_of(72 * core, 8), 72)
    for half in range(2):
        wg_ref[:, pl.ds(128 * half, 128)] = fin[half, rows, :]

    for i2 in range(ROWS):
        ig_copy(i2).wait()
    for index in range(8):
        if moves[index][0] == 0:
            halo(index).wait_send()
        else:
            @pl.when(can_send(index))
            def _():
                halo(index).wait_send()
    for side in range(2):
        @pl.when(has_down if side == 0 else has_up)
        def _():
            v_halo(side).wait_send()

    @pl.when(north)
    def _():
        y_halo(6).wait_send()

    @pl.when(south)
    def _():
        y_halo(0).wait_send()

    @pl.when(polar_dev)
    def _():
        for dc in range(2):
            for step in range(N_LON):
                if dc or step:
                    gs_copy(dc, step).wait_send()

    for group in range(len(GROUPS)):
        twin_copy(group).wait_send()
        for step in range(1, N_LON):
            lon_copy(group, step).wait_send()
    for k in range(K):
        for b in range(2):
            owner, copy = granule(k, b)

            @pl.when(owner != p)
            def _():
                copy.wait_send()
    for b in range(2):
        e, valid = place(b)
        for dc in range(2):
            @pl.when(valid & needed(e, 1 - core if dc else core))
            def _():
                for step in range(N_LON):
                    if dc or step:
                        final_copy(b, e, dc, step).wait_send()


def filter_rows(filt, widths, offsets):
    span = jnp.arange(2 * REACH + 1, dtype=jnp.int32) - REACH
    keep = jnp.abs(span)[None, :] <= widths[:, None]
    masked = jnp.where(keep[None, :, None, :], filt, jnp.zeros_like(filt))[..., ::-1]
    pieces = []
    for n in range(CANDS):
        picked = jnp.zeros((K, ROWS, 2 * REACH + 1), BF16)
        for r in range(3):
            hit = (offsets == 2 - n - r)[None, :, None]
            picked = jnp.where(hit, masked[:, :, r], picked)
        moved = jnp.transpose(picked, (1, 0, 2))
        lanes = WIN - 2 * REACH - 1 + (DEPTH - CANDS * WIN if n == CANDS - 1 else 0)
        pieces.append(jnp.pad(moved, ((4 - n, n), (0, 16 - K), (0, lanes))))
    return jnp.concatenate(pieces, axis=2)


def circle_rows(zonal_weight, offsets, polar_rows):
    lat = lax.axis_index("lat")
    pole = lat // (N_LAT // 2)
    own = lax.dynamic_slice_in_dim(zonal_weight, lax.axis_index("lon") * LONS, LONS, 3)
    mine = lax.dynamic_slice_in_dim(polar_rows, 2 * pole, 2) - lat * ROWS
    slot = jnp.arange(8, dtype=jnp.int32) - 2
    row = jnp.arange(ROWS, dtype=jnp.int32)
    band = jnp.arange(3, dtype=jnp.int32)
    hit = (row[None, :] == mine[:, None])[None, :, :, None] & (
        (slot[:, None] - row[None, :] - offsets[None, :])[:, None, :, None] == band
    )
    picked = jnp.einsum("sqir,kirj->sqkj", hit.astype(BF16), own, preferred_element_type=F32)
    return jnp.pad(picked.astype(BF16), ((0, 0), (0, 0), (0, 16 - K), (0, 0))).reshape(8, 32, LONS)


def body(input_field, grad_out, weight, filt, zonal_weight, widths, offsets, polar_rows):
    values = filter_rows(filt, widths, offsets)
    circle = circle_rows(zonal_weight, offsets, polar_rows)
    dma = pltpu.SemaphoreType.DMA
    anywhere = pl.BlockSpec(memory_space=pl.ANY)
    vmem = pl.BlockSpec(memory_space=pltpu.VMEM)
    groups = len(GROUPS)
    return pl.pallas_call(
        kernel,
        out_shape=(
            jax.ShapeDtypeStruct((ROWS, LONS, C), BF16),
            jax.ShapeDtypeStruct((72, C), F32),
        ),
        in_specs=[anywhere, anywhere, anywhere, vmem, vmem, pl.BlockSpec(memory_space=pltpu.SMEM)],
        out_specs=(anywhere, vmem),
        scratch_shapes=[
            pltpu.VMEM((8, LONS + 2 * REACH, C), BF16),
            pltpu.VMEM((ROWS, LONS, C), BF16),
            pltpu.VMEM((C, ROWS * LONS), BF16),
            pltpu.VMEM((K * C, C), BF16),
            pltpu.VMEM((K * C, C), BF16),
            pltpu.VMEM((2, 2, 16, DEPTH), BF16),
            pltpu.VMEM((2, 32, LONS), BF16),
            pltpu.VMEM((ROWS * 16, DEPTH), F32),
            pltpu.VMEM((ROWS, K * JB, DEPTH), BF16),
            pltpu.VMEM((ROWS * LONS, K * C), BF16),
            pltpu.VMEM((ROWS, 32, LONS), BF16),
            pltpu.VMEM((32, C), F32),
            pltpu.VMEM((C, 32), F32),
            pltpu.VMEM((8, C), F32),
            pltpu.VMEM((N_LON, 8, C), F32),
            pltpu.VMEM((8, C), F32),
            pltpu.VMEM((K, C, 128), F32),
            pltpu.VMEM((K, C, 128), BF16),
            pltpu.VMEM((K, C, 128), BF16),
            pltpu.VMEM((K, C, 128), BF16),
            pltpu.VMEM((N_LON, K, 32, 128), BF16),
            pltpu.VMEM((K, 2, 16, 128), BF16),
            pltpu.VMEM((2, N_P, 16, 128), BF16),
            pltpu.VMEM((2, 16, 128), F32),
            pltpu.VMEM((2, 144, 128), F32),
            pltpu.VMEM((ROWS, LONS, C), BF16),
            dma((3,)), dma((8,)), dma((8,)), dma((2,)), dma((2,)), dma, dma, dma((2, N_LON)), dma,
            dma((groups,)), dma((groups,)), dma((groups, N_LON)), dma((groups,)),
            dma((K, 2)), dma((2,)), dma((2, 2, N_LON)), dma, dma((ROWS,)),
        ],
        compiler_params=pltpu.CompilerParams(
            collective_id=0, has_side_effects=True, vmem_limit_bytes=48 * 1024 * 1024
        ),
        name="sphere_backward",
    )(grad_out, input_field, weight, values, circle, polar_rows)


def solution(mesh):
    in_specs = (
        P("lat", "lon", None),
        P("lat", "lon", None),
        P(),
        P(None, "lat", None, None),
        P(None, "lat", None, None),
        P("lat"),
        P("lat"),
        P(),
    )
    out_specs = (P("lat", "lon", None), P("lat", None))
    return jax.shard_map(body, mesh=mesh, in_specs=in_specs, out_specs=out_specs, check_vma=False)
```

profile of v0, /device:TPU:1, one launch (start us, length us, event | category | flops | bytes accessed | tf_op | source)
XLA Modules:
  0.0 57.3 jit_solution(9834252656355011080)
XLA Ops:
  0.6 0.0 copy-start
  0.6 0.0 copy-start.4
  0.7 0.0 copy-start.1
  0.7 0.8 %dynamic-slice_subtract_fusion = s32[2]{0:T(128)S(1)} fusion(s32[4]{0:T(128)} %polar_ref.1, s32[]{:T(128)S(6)} %select_n.78, s32[]{:T(128)S(6)} %mul.10), kind=kLoop, calls=%fused_computation.34 | loop fusion | flops 2 | bytes 24 | tf_op jit(solution)/shard_map/sub | solution.py:471
  1.5 0.1 iota_compare_fusion.1
  1.6 0.7 %broadcast_compare_fusion = pred[4,33]{1,0:T(4,128)(4,1)S(1)} fusion(s32[33]{0:T(128)S(1)} %add_abs_fusion, s32[4]{0:T(128)} %param.13), kind=kLoop, calls=%fused_computation.32 | loop fusion | flops 132 | bytes 280 | tf_op jit(solution)/shard_map/le | solution.py:453
  2.3 0.7 %subtract_subtract_fusion = s32[8,4]{0,1:T(4,128)S(1)} fusion(s32[4]{0:T(128)} %param.14, s32[8]{0:T(128)S(1)} %iota_add_fusion), kind=kLoop, calls=%fused_computation.30 | loop fusion | flops 64 | bytes 176 | tf_op jit(solution)/shard_map/sub | solution.py:476
  3.1 0.7 %broadcast_compare_fusion.1 = (pred[4]{0:T(512)(128)(4,1)S(1)}, pred[4]{0:T(512)(128)(4,1)S(1)}, pred[4]{0:T(512)(128)(4,1)S(1)}, pred[4]{0:T(512)(128)(4,1)S(1)...) fusion(s32[4]{0:T(128)} %param.14), kind=kLoop, calls=%fused_computation.36 | loop fusion | flops 28 | bytes 44 | tf_op jit(solution)/shard_map/eq | solution.py:459
  3.7 0.8 %copy_select_fusion = bf16[9,4,3,33]{3,0,1,2:T(8,128)(2,1)S(1)} fusion(bf16[9,4,3,33]{3,1,2,0:T(4,128)(2,1)} %param.11, pred[4,33]{1,0:T(4,128)(4,1)S(1)} %broadcast_compare_fusion), kind=kLoop, calls=%fused_computation.4 | loop fusion | flops 3564 | bytes 14388 | tf_op jit(solution)/shard_map/jit(_where)/select_n | solution.py:454
  4.5 0.1 slice.31
  4.6 0.1 slice.35
  4.7 0.1 slice.33
  4.8 0.1 fusion.17
  5.0 0.1 concatenate.3.v_ref
  5.1 0.0 copy-done
  5.1 0.3 fusion
  5.5 0.0 copy-done.4
  5.5 0.0 copy-done.1
  5.5 0.0 copy-start.2
  5.5 1.0 %copy-done.2 = bf16[4,256,256]{2,1,0:T(8,128)(2,1)S(1)} copy-done((bf16[4,256,256]{2,1,0:T(8,128)(2,1)S(1)}, bf16[4,256,256]{2,1,0:T(8,128)(2,1)}, u32[]{:S(2)}) %copy-start.2) | copy-done | bytes 524312
  6.5 0.0 copy-start.3
  6.6 1.0 %copy-done.3 = bf16[4,256,256]{2,1,0:T(8,128)(2,1)S(1)} copy-done((bf16[4,256,256]{2,1,0:T(8,128)(2,1)S(1)}, bf16[4,256,256]{2,1,0:T(8,128)(2,1)}, u32[]{:S(2)}) %copy-start.3) | copy-done | bytes 524312
  7.6 48.3 %sphere_backward.1 = (bf16[4,256,256]{2,1,0:T(8,128)(2,1)S(1)}, f32[72,256]{1,0:T(8,128)S(1)}) custom-call(bf16[4,256,256]{2,1,0:T(8,128)(2,1)S(1)} %copy-done.2, bf16[4,256,256]{2,1,0:T(8,128)(2,1)S(1)} %copy-done.3, bf16[2304,256]{1,0:T(8,128)(2,1)S(1)} %copy-done.1, bf16[8,16,512]{2,1,0:T(8,128)(2,1)S(1)} %concatenate.3.v_ref, ...), custom_call_target="tpu_custom_call" | custom-call | tf_op jit(solution)/shard_map/sphere_backward/pallas_call | solution.py:489
  55.9 0.8 %copy.18 = bf16[4,256,256]{2,1,0:T(8,128)(2,1)} copy(bf16[4,256,256]{2,1,0:T(8,128)(2,1)S(1)} %get-tuple-element.19) | data formatting | bytes 1048576
  56.7 0.6 %copy.19 = f32[72,256]{1,0:T(8,128)} copy(f32[72,256]{1,0:T(8,128)S(1)} %get-tuple-element.20) | data formatting | bytes 147456
  (11 shorter events, 0.1 us)
Async XLA Ops:
  0.6 4.5 %copy-start = (bf16[9,4,3,2048]{3,1,2,0:T(4,128)(2,1)S(1)}, bf16[9,4,3,2048]{3,1,2,0:T(4,128)(2,1)}, u32[]{:S(2)}) copy-start(bf16[9,4,3,2048]{3,1,2,0:T(4,128)(2,1)} %param.12) | copy-start | bytes 1327108
  0.6 4.8 %copy-start.4 = (s32[4]{0:T(128)S(1)}, s32[4]{0:T(128)}, u32[]{:S(2)}) copy-start(s32[4]{0:T(128)} %polar_ref.1) | copy-start | bytes 52
  0.7 4.8 %copy-start.1 = (bf16[2304,256]{1,0:T(8,128)(2,1)S(1)}, bf16[2304,256]{1,0:T(8,128)(2,1)}, u32[]{:S(2)}) copy-start(bf16[2304,256]{1,0:T(8,128)(2,1)} %w_hbm.1) | copy-start | bytes 3538948
  5.5 1.0 %copy-start.2 = (bf16[4,256,256]{2,1,0:T(8,128)(2,1)S(1)}, bf16[4,256,256]{2,1,0:T(8,128)(2,1)}, u32[]{:S(2)}) copy-start(bf16[4,256,256]{2,1,0:T(8,128)(2,1)} %g_hbm.1) | copy-start | bytes 1572868
  6.5 1.0 %copy-start.3 = (bf16[4,256,256]{2,1,0:T(8,128)(2,1)S(1)}, bf16[4,256,256]{2,1,0:T(8,128)(2,1)}, u32[]{:S(2)}) copy-start(bf16[4,256,256]{2,1,0:T(8,128)(2,1)} %x_hbm.1) | copy-start | bytes 1572868
where the time goes:
time: 57.8 us; the launch traced here: 57.3 us
  Pallas kernels  48.3 us (84%)
  local copies, waits for them, and re-layouts  4 us (7%)
  other arithmetic  3.91 us (7%)
  between operations  0.81 us (1%)
    pallas_call x1, Pallas kernels, body(): pl.pallas_call(kernel, out_shape=(jax.ShapeDtypeStruct((ROWS, LONS, C), B...  48.3 us
    unnamed x13, local copies, waits for them, and re-layouts  3.55 us

commit v1 on v0

--- a/solution.py
+++ b/solution.py
@@ -32,9 +32,9 @@
 
 
 def kernel(
-    g_hbm, x_hbm, w_hbm, v_ref, y_ref, polar_ref,
+    g_hbm, x_hbm, w_hbm, filt_ref, z_hbm, width_ref, offset_ref, polar_ref,
     ig_hbm, wg_ref,
-    gx, xv, xt, wv, wt, vh, yh, vf, tt, hh, yy, ztf, zst, gs_own, gs_buf, gsel,
+    gx, xv, xt, wv, wt, lv, vown, vh, vf, tt, hh, zv, zs, yf, yown, yh, yy, ztf, zst, gs_own, gs_buf, gsel,
     wown, wsnd, cx, s1, rb, s2, pr, s3, fin, igv,
     loc_sem, halo_send, halo_recv, vsend, vrecv, ysend, yrecv, gs_send, gs_sem,
     cs_send, cs_recv, ls_send, ls_recv, ps_send, ps_recv, fs_send, fs_recv, out_sem,
@@ -48,19 +48,30 @@
     def lon_at(step):
         return lax.rem(lon + step, N_LON)
 
-    def remote(src, dst, send, recv, to_lat, to_lon):
+    def remote(src, dst, send, recv, to_lat, to_lon, tag="rs"):
         return pltpu.make_async_remote_copy(
             src_ref=src, dst_ref=dst, send_sem=send, recv_sem=recv,
             device_id={"lat": to_lat, "lon": to_lon}, device_id_type=MESH,
         )
 
+    north, south = lat == 0, lat == N_LAT - 1
+    polar_dev = north | south
+    affected = polar_dev | (lat == 1) | (lat == N_LAT - 2)
+
     g_copy = pltpu.make_async_copy(g_hbm, gx.at[pl.ds(2, ROWS), pl.ds(REACH, LONS)], loc_sem.at[0])
     x_copy = pltpu.make_async_copy(x_hbm, xv, loc_sem.at[1])
     w_copy = pltpu.make_async_copy(w_hbm, wv, loc_sem.at[2])
+    z_copy = pltpu.make_async_copy(
+        z_hbm.at[:, :, :, pl.ds(pl.multiple_of(lon * LONS, LONS), LONS)], zv, loc_sem.at[3]
+    )
     g_copy.start()
     x_copy.start()
     w_copy.start()
 
+    @pl.when(polar_dev)
+    def _():
+        z_copy.start()
+
     barrier = pltpu.get_barrier_semaphore()
 
     def greet(to_lat, to_lon):
@@ -74,20 +85,47 @@
         for step in (0, 1, N_LON - 1):
             greet(outer, lon_at(step))
 
+    for step in range(1, N_P):
+        greet(2 * lax.rem(p + step, N_P) + core, lon)
     for step in range(1, N_LON):
         greet(lat, lon_at(step))
     for step in range(N_LON):
         greet(twin, lon_at(step))
-    for step in range(1, N_P):
-        greet(2 * lax.rem(p + step, N_P) + core, lon)
+
+    span = 2 * REACH + 1
+    row_i = lax.broadcasted_iota(jnp.int32, (ROWS, span), 0)
+    tap = lax.broadcasted_iota(jnp.int32, (ROWS, span), 1)
+    offset_v = jnp.zeros((ROWS, span), jnp.int32)
+    width_v = jnp.zeros((ROWS, span), jnp.int32)
+    for i in range(ROWS):
+        offset_v = jnp.where(row_i == i, offset_ref[i], offset_v)
+        width_v = jnp.where(row_i == i, width_ref[i], width_v)
+    keep = jnp.abs(tap - REACH) <= width_v
+    choose = {m: jnp.where(keep & (offset_v == 2 - m), 1.0, 0.0) for m in (2, 3, 4)}
+    lv[...] = jnp.zeros_like(lv)
+    for k in range(K):
+        values = [filt_ref[k, r].astype(F32) for r in range(3)]
+        for n in range(CANDS):
+            terms = [choose[n + r] * values[r] for r in range(3) if n + r in choose]
+            lv[n, pl.ds((4 - n) * 16 + k, ROWS, stride=16), :] = functools.reduce(jnp.add, terms)
+    tap = lax.broadcasted_iota(jnp.int32, (span, DEPTH), 0)
+    lane = lax.broadcasted_iota(jnp.int32, (span, DEPTH), 1)
+    placed = jnp.zeros((128, DEPTH), F32)
+    for n in range(CANDS):
+        where = jnp.where(lane + tap == WIN * n + 2 * REACH, 1.0, 0.0).astype(BF16)
+        placed = placed + dot(lv[n].astype(BF16), where)
+    vown[...] = placed.astype(BF16).reshape(8, 16, DEPTH)
+
     pl.semaphore_wait(barrier, 2 * N_LON + N_P - 2 + 3 * has_outer.astype(jnp.int32))
 
     up, down = lat - 1, lat + 1
     has_up, has_down = lat > 0, lat < N_LAT - 1
-    left, right = lon_at(N_LON - 1), lon_at(1)
     rows_of = {-1: (0, 2, 6), 0: (0, ROWS, 2), 1: (2, 2, 0)}
     cols_of = {-1: (0, REACH, REACH + LONS), 0: (0, LONS, REACH), 1: (LONS - REACH, REACH, 0)}
-    moves = [(1, 0), (-1, 0), (0, 1), (0, -1), (1, 1), (1, -1), (-1, 1), (-1, -1)]
+    moves = [(1, 0), (-1, 0), (1, 1), (1, -1), (-1, 1), (-1, -1), (0, 1), (0, -1)]
+    from_up = [index for index in range(8) if moves[index][0] == 1]
+    from_down = [index for index in range(8) if moves[index][0] == -1]
+    level = [index for index in range(8) if moves[index][0] == 0]
 
     def halo(index):
         dlat, dlon = moves[index]
@@ -97,53 +135,41 @@
             g_hbm.at[pl.ds(r0, rn), pl.ds(c0, cn)],
             gx.at[pl.ds(r_to, rn), pl.ds(c_to, cn)],
             halo_send.at[index], halo_recv.at[index],
-            lat + dlat, lon_at(dlon % N_LON),
+            lat + dlat, lon_at(dlon % N_LON), "halo",
         )
 
-    def can_send(index):
-        dlat = moves[index][0]
-        return has_down if dlat == 1 else has_up
-
-    def can_recv(index):
-        dlat = moves[index][0]
-        return has_up if dlat == 1 else has_down
-
     def v_halo(side):
-        src = v_ref.at[pl.ds(6, 2)] if side == 0 else v_ref.at[pl.ds(0, 2)]
-        return remote(src, vh.at[side], vsend.at[side], vrecv.at[side], down if side == 0 else up, lon)
-
-    for side in range(2):
-        @pl.when(has_down if side == 0 else has_up)
-        def _():
-            v_halo(side).start()
-
-    for index in range(8):
-        if moves[index][0] == 0:
+        src = vown.at[pl.ds(6, 2)] if side == 0 else vown.at[pl.ds(0, 2)]
+        return remote(src, vh.at[side], vsend.at[side], vrecv.at[side], down if side == 0 else up, lon, "halo")
+
+    @pl.when(has_down)
+    def _():
+        v_halo(0).start()
+        for index in from_up:
             halo(index).start()
-        else:
-            @pl.when(can_send(index))
-            def _():
-                halo(index).start()
-
-    north, south = lat == 0, lat == N_LAT - 1
-    polar_dev = north | south
-    affected = polar_dev | (lat == 1) | (lat == N_LAT - 2)
+
+    @pl.when(has_up)
+    def _():
+        v_halo(1).start()
+        for index in from_down:
+            halo(index).start()
+
+    for index in level:
+        halo(index).start()
+
+    g_copy.wait()
+
+    def gs_copy(dc, step):
+        return remote(
+            gs_own, gs_buf.at[lon], gs_send.at[dc, step], gs_sem, twin if dc else lat, lon_at(step), "halo"
+        )
 
     def y_halo(first):
-        return remote(y_ref.at[pl.ds(first, 2)], yh, ysend, yrecv, twin, lon)
-
-    @pl.when(north)
-    def _():
-        y_halo(6).start()
-
-    @pl.when(south)
-    def _():
-        y_halo(0).start()
-
-    g_copy.wait()
-
-    def gs_copy(dc, step):
-        return remote(gs_own, gs_buf.at[lon], gs_send.at[dc, step], gs_sem, twin if dc else lat, lon_at(step))
+        return remote(yown.at[pl.ds(first, 2)], yh, ysend, yrecv, twin, lon, "halo")
+
+    @pl.when(jnp.logical_not(polar_dev))
+    def _():
+        yown[...] = jnp.zeros_like(yown)
 
     @pl.when(polar_dev)
     def _():
@@ -157,13 +183,44 @@
                 if dc or step:
                     gs_copy(dc, step).start()
         pltpu.make_async_copy(gs_own, gs_buf.at[lon], gs_sem).start()
-
-    @pl.when(lat == 0)
+        pole = lax.div(lat, N_LAT // 2)
+        entry = lax.broadcasted_iota(jnp.int32, (16, 16), 0)
+        source = lax.broadcasted_iota(jnp.int32, (16, 16), 1)
+        row = source & 3
+        first_q = polar_ref[2 * pole] - lat * ROWS
+        second_q = polar_ref[2 * pole + 1] - lat * ROWS
+        polar_row = jnp.where((entry & 1) == 0, first_q, second_q)
+        moved = row + (source >> 2)
+        for i in range(ROWS):
+            moved = moved + jnp.where(row == i, offset_ref[i], 0)
+        hit = (row == polar_row) & (moved == (entry >> 1) - 2) & (source < 12)
+        z_copy.wait()
+        zs[pl.ds(8, 8), :] = jnp.zeros((8, K * LONS), F32)
+        for k in range(K):
+            for r in range(3):
+                zs[pl.ds(4 * r, 4), pl.ds(k * LONS, LONS)] = zv[k, r].astype(F32)
+        picked = dot(jnp.where(hit, 1.0, 0.0).astype(BF16), zs[...].astype(BF16))
+        yf[...] = jnp.zeros_like(yf)
+        for k in range(K):
+            for half in range(2):
+                yf[half, pl.ds(k, 16, stride=16), :] = picked[:, k * LONS + 128 * half:k * LONS + 128 * half + 128]
+        for half in range(2):
+            yown[:, :, pl.ds(128 * half, 128)] = yf[half].astype(BF16).reshape(8, 32, 128)
+
+    @pl.when(north)
+    def _():
+        y_halo(6).start()
+
+    @pl.when(south)
+    def _():
+        y_halo(0).start()
+
+    @pl.when(north)
     def _():
         gx[pl.ds(0, 2)] = jnp.zeros((2,) + gx.shape[1:], BF16)
         vh[0] = jnp.zeros(vh.shape[1:], BF16)
 
-    @pl.when(lat == N_LAT - 1)
+    @pl.when(south)
     def _():
         gx[pl.ds(6, 2)] = jnp.zeros((2,) + gx.shape[1:], BF16)
         vh[1] = jnp.zeros(vh.shape[1:], BF16)
@@ -180,24 +237,68 @@
 
     lax.fori_loop(0, K, turn, 0)
 
-    for side in range(2):
-        @pl.when(has_up if side == 0 else has_down)
-        def _():
-            v_halo(side).wait_recv()
+    def band_rows(base, side):
+        for a in range(2):
+            vf[pl.ds(16 * a, 16), :] = vown[2 + base + a].astype(F32) + vh[side, a].astype(F32)
+
+        def band(k, carry):
+            for a in range(2):
+                row = jnp.broadcast_to(vf[pl.ds(16 * a + k, 1), :], (JB, DEPTH))
+                rolled = pltpu.roll(row, 0, 1, stride=1, stride_axis=0)
+                tt[base + a, pl.ds(pl.multiple_of(k * JB, JB), JB), :] = rolled.astype(BF16)
+            return carry
+
+        lax.fori_loop(0, K, band, 0)
+
+    def spread_rows(base, k0, k1):
+        def spread(step, carry):
+            for half in range(2):
+                index = 2 * step + half
+                i2, jb = base + lax.div(index, LONS // JB), lax.rem(index, LONS // JB)
+                at = pl.ds(pl.multiple_of(jb * JB, JB), WIN)
+                windows = [gx[i2 + n, at, :] for n in range(CANDS)]
+                windows.append(jnp.zeros((DEPTH - CANDS * WIN, C), BF16))
+                moved = dot(tt[i2, pl.ds(k0 * JB, (k1 - k0) * JB)], jnp.concatenate(windows, axis=0)).astype(BF16)
+                rows = pl.ds(pl.multiple_of(i2 * LONS + jb * JB, JB), JB)
+                for k in range(k0, k1):
+                    hh[rows, pl.ds(k * C, C)] = moved[(k - k0) * JB:(k - k0 + 1) * JB]
+            return carry
+
+        lax.fori_loop(0, LONS // JB, spread, 0)
+
+    near, far = 2 - 2 * core, 2 * core
+
+    def arrive(index_list):
+        for index in index_list:
+            halo(index).wait_recv()
+
+    arrive(level)
+
+    @pl.when(core == 0)
+    def _():
+        v_halo(1).wait_recv()
+        arrive(from_down)
+
+    @pl.when(core == 1)
+    def _():
+        v_halo(0).wait_recv()
+        arrive(from_up)
+
+    band_rows(near, 1 - core)
+    spread_rows(near, 0, K)
+
+    @pl.when((core == 0) & has_up)
+    def _():
+        v_halo(0).wait_recv()
+
+    @pl.when((core == 1) & has_down)
+    def _():
+        v_halo(1).wait_recv()
+
+    band_rows(far, core)
+
     for i2 in range(ROWS):
-        vf[pl.ds(16 * i2, 16), :] = v_ref[2 + i2].astype(F32) + vh[i2 // 2, i2 % 2].astype(F32)
-
-    def band(index, carry):
-        i2, k = lax.div(index, K), lax.rem(index, K)
-        row = jnp.broadcast_to(vf[pl.ds(16 * i2 + k, 1), :], (JB, DEPTH))
-        rolled = pltpu.roll(row, 0, 1, stride=1, stride_axis=0)
-        tt[i2, pl.ds(pl.multiple_of(k * JB, JB), JB), :] = rolled.astype(BF16)
-        return carry
-
-    lax.fori_loop(0, ROWS * K, band, 0)
-
-    for i2 in range(ROWS):
-        yy[i2] = y_ref[2 + i2]
+        yy[i2] = yown[2 + i2]
 
     @pl.when(lat == 1)
     def _():
@@ -244,26 +345,13 @@
         for q in range(2):
             ztf[pl.ds(16 * q + k, 1), :] = mixed[q:q + 1]
 
-    for index in range(8):
-        if moves[index][0] == 0:
-            halo(index).wait_recv()
-        else:
-            @pl.when(can_recv(index))
-            def _():
-                halo(index).wait_recv()
-
-    def spread(index, carry):
-        i2, jb = lax.div(index, LONS // JB), lax.rem(index, LONS // JB)
-        at = pl.ds(pl.multiple_of(jb * JB, JB), WIN)
-        windows = [gx[i2 + n, at, :] for n in range(CANDS)]
-        windows.append(jnp.zeros((DEPTH - CANDS * WIN, C), BF16))
-        moved = dot(tt[i2], jnp.concatenate(windows, axis=0)).astype(BF16)
-        rows = pl.ds(pl.multiple_of(index * JB, JB), JB)
-        for k in range(K):
-            hh[rows, pl.ds(k * C, C)] = moved[k * JB:(k + 1) * JB]
-        return carry
-
-    lax.fori_loop(0, ROWS * LONS // JB, spread, 0)
+    @pl.when((core == 0) & has_up)
+    def _():
+        arrive(from_up)
+
+    @pl.when((core == 1) & has_down)
+    def _():
+        arrive(from_down)
 
     def twin_copy(group):
         k0, k1 = GROUPS[group]
@@ -372,45 +460,43 @@
     z_low = (circle_total - z_high.astype(F32)).astype(BF16)
     z_parts = jnp.concatenate([z_high, z_low], axis=0)
 
-    def pull(i2):
-        grad = dot(hh[pl.ds(i2 * LONS, LONS), :], wt[...])
-        twice = jnp.concatenate([yy[i2], yy[i2]], axis=0)
-        igv[i2] = (grad + dot(twice, z_parts, 0, 0)).astype(BF16)
-        ig_copy(i2).start()
-
+    def pull(half):
+        grad = dot(hh[pl.ds(half * 2 * LONS, 2 * LONS), :], wt[...])
+        for a in range(2):
+            i2 = 2 * half + a
+            twice = jnp.concatenate([yy[i2], yy[i2]], axis=0)
+            igv[i2] = (grad[a * LONS:(a + 1) * LONS] + dot(twice, z_parts, 0, 0)).astype(BF16)
+            ig_copy(i2).start()
+
+    spread_rows(far, *GROUPS[0])
     mix(0)
+    spread_rows(far, *GROUPS[1])
     mix(1)
     over_lon(0)
+    spread_rows(far, *GROUPS[2])
     mix(2)
     over_lon(1)
     over_lat(0)
-    pull(0)
     over_lon(2)
     over_lat(1)
+    pull(0)
+    over_lat(2)
     pull(1)
-    over_lat(2)
-    pull(2)
     spread_out()
-    pull(3)
-    some = fin.at[:, pl.ds(0, 80)]
-    pltpu.make_async_copy(some, some, fs_recv).wait()
-    rows = pl.ds(pl.multiple_of(72 * core, 8), 72)
-    for half in range(2):
-        wg_ref[:, pl.ds(128 * half, 128)] = fin[half, rows, :]
-
-    for i2 in range(ROWS):
-        ig_copy(i2).wait()
-    for index in range(8):
-        if moves[index][0] == 0:
+    for index in level:
+        halo(index).wait_send()
+
+    @pl.when(has_down)
+    def _():
+        v_halo(0).wait_send()
+        for index in from_up:
             halo(index).wait_send()
-        else:
-            @pl.when(can_send(index))
-            def _():
-                halo(index).wait_send()
-    for side in range(2):
-        @pl.when(has_down if side == 0 else has_up)
-        def _():
-            v_halo(side).wait_send()
+
+    @pl.when(has_up)
+    def _():
+        v_halo(1).wait_send()
+        for index in from_down:
+            halo(index).wait_send()
 
     @pl.when(north)
     def _():
@@ -438,6 +524,12 @@
             @pl.when(owner != p)
             def _():
                 copy.wait_send()
+    some = fin.at[:, pl.ds(0, 80)]
+    pltpu.make_async_copy(some, some, fs_recv).wait()
+    rows = pl.ds(pl.multiple_of(72 * core, 8), 72)
+    for half in range(2):
+        wg_ref[:, pl.ds(128 * half, 128)] = fin[half, rows, :]
+
     for b in range(2):
         e, valid = place(b)
         for dc in range(2):
@@ -446,45 +538,15 @@
                 for step in range(N_LON):
                     if dc or step:
                         final_copy(b, e, dc, step).wait_send()
-
-
-def filter_rows(filt, widths, offsets):
-    span = jnp.arange(2 * REACH + 1, dtype=jnp.int32) - REACH
-    keep = jnp.abs(span)[None, :] <= widths[:, None]
-    masked = jnp.where(keep[None, :, None, :], filt, jnp.zeros_like(filt))[..., ::-1]
-    pieces = []
-    for n in range(CANDS):
-        picked = jnp.zeros((K, ROWS, 2 * REACH + 1), BF16)
-        for r in range(3):
-            hit = (offsets == 2 - n - r)[None, :, None]
-            picked = jnp.where(hit, masked[:, :, r], picked)
-        moved = jnp.transpose(picked, (1, 0, 2))
-        lanes = WIN - 2 * REACH - 1 + (DEPTH - CANDS * WIN if n == CANDS - 1 else 0)
-        pieces.append(jnp.pad(moved, ((4 - n, n), (0, 16 - K), (0, lanes))))
-    return jnp.concatenate(pieces, axis=2)
-
-
-def circle_rows(zonal_weight, offsets, polar_rows):
-    lat = lax.axis_index("lat")
-    pole = lat // (N_LAT // 2)
-    own = lax.dynamic_slice_in_dim(zonal_weight, lax.axis_index("lon") * LONS, LONS, 3)
-    mine = lax.dynamic_slice_in_dim(polar_rows, 2 * pole, 2) - lat * ROWS
-    slot = jnp.arange(8, dtype=jnp.int32) - 2
-    row = jnp.arange(ROWS, dtype=jnp.int32)
-    band = jnp.arange(3, dtype=jnp.int32)
-    hit = (row[None, :] == mine[:, None])[None, :, :, None] & (
-        (slot[:, None] - row[None, :] - offsets[None, :])[:, None, :, None] == band
-    )
-    picked = jnp.einsum("sqir,kirj->sqkj", hit.astype(BF16), own, preferred_element_type=F32)
-    return jnp.pad(picked.astype(BF16), ((0, 0), (0, 0), (0, 16 - K), (0, 0))).reshape(8, 32, LONS)
+    for i2 in range(ROWS):
+        ig_copy(i2).wait()
 
 
 def body(input_field, grad_out, weight, filt, zonal_weight, widths, offsets, polar_rows):
-    values = filter_rows(filt, widths, offsets)
-    circle = circle_rows(zonal_weight, offsets, polar_rows)
     dma = pltpu.SemaphoreType.DMA
-    anywhere = pl.BlockSpec(memory_space=pl.ANY)
+    hbm = pl.BlockSpec(memory_space=pltpu.HBM)
     vmem = pl.BlockSpec(memory_space=pltpu.VMEM)
+    smem = pl.BlockSpec(memory_space=pltpu.SMEM)
     groups = len(GROUPS)
     return pl.pallas_call(
         kernel,
@@ -492,19 +554,25 @@
             jax.ShapeDtypeStruct((ROWS, LONS, C), BF16),
             jax.ShapeDtypeStruct((72, C), F32),
         ),
-        in_specs=[anywhere, anywhere, anywhere, vmem, vmem, pl.BlockSpec(memory_space=pltpu.SMEM)],
-        out_specs=(anywhere, vmem),
+        in_specs=[hbm, hbm, hbm, vmem, hbm, smem, smem, smem],
+        out_specs=(pl.BlockSpec(memory_space=pl.ANY), vmem),
         scratch_shapes=[
             pltpu.VMEM((8, LONS + 2 * REACH, C), BF16),
             pltpu.VMEM((ROWS, LONS, C), BF16),
             pltpu.VMEM((C, ROWS * LONS), BF16),
             pltpu.VMEM((K * C, C), BF16),
             pltpu.VMEM((K * C, C), BF16),
+            pltpu.VMEM((CANDS, 128, 2 * REACH + 1), F32),
+            pltpu.VMEM((8, 16, DEPTH), BF16),
             pltpu.VMEM((2, 2, 16, DEPTH), BF16),
-            pltpu.VMEM((2, 32, LONS), BF16),
-            pltpu.VMEM((ROWS * 16, DEPTH), F32),
+            pltpu.VMEM((32, DEPTH), F32),
             pltpu.VMEM((ROWS, K * JB, DEPTH), BF16),
             pltpu.VMEM((ROWS * LONS, K * C), BF16),
+            pltpu.VMEM((K, 3, ROWS, LONS), BF16),
+            pltpu.VMEM((16, K * LONS), F32),
+            pltpu.VMEM((2, 256, 128), F32),
+            pltpu.VMEM((8, 32, LONS), BF16),
+            pltpu.VMEM((2, 32, LONS), BF16),
             pltpu.VMEM((ROWS, 32, LONS), BF16),
             pltpu.VMEM((32, C), F32),
             pltpu.VMEM((C, 32), F32),
@@ -521,15 +589,18 @@
             pltpu.VMEM((2, 16, 128), F32),
             pltpu.VMEM((2, 144, 128), F32),
             pltpu.VMEM((ROWS, LONS, C), BF16),
-            dma((3,)), dma((8,)), dma((8,)), dma((2,)), dma((2,)), dma, dma, dma((2, N_LON)), dma,
+            dma((4,)), dma((8,)), dma((8,)), dma((2,)), dma((2,)), dma, dma, dma((2, N_LON)), dma,
             dma((groups,)), dma((groups,)), dma((groups, N_LON)), dma((groups,)),
             dma((K, 2)), dma((2,)), dma((2, 2, N_LON)), dma, dma((ROWS,)),
         ],
         compiler_params=pltpu.CompilerParams(
-            collective_id=0, has_side_effects=True, vmem_limit_bytes=48 * 1024 * 1024
+            collective_id=0, has_side_effects=True, vmem_limit_bytes=60 * 1024 * 1024
         ),
         name="sphere_backward",
-    )(grad_out, input_field, weight, values, circle, polar_rows)
+    )(
+        grad_out, input_field, weight, jnp.transpose(filt, (0, 2, 1, 3)),
+        jnp.transpose(zonal_weight, (0, 2, 1, 3)), widths, offsets, polar_rows,
+    )
 
 
 def solution(mesh):

time: 57.8 us -> 53.2 us (0.920)
  other arithmetic: 3.91 us -> 0 us
  local copies, waits for them, and re-layouts: 4 us -> 3.39 us
  Pallas kernels: 48.3 us -> 48.9 us
    sub x3 -> x0, other arithmetic: 1.57 us -> none  [the longest x1 0.85 us: circle_rows(): mine = lax.dynamic_slice_in_dim(polar_rows, 2 * pole, 2) - lat * ROWS]
    select_n x1 -> x0, other arithmetic: 0.76 us -> none  [filter_rows(): jnp.where(keep[None, :, None, :], filt, jnp.zeros_like(filt))[..., ::-1]]
    eq x3 -> x0, other arithmetic: 0.74 us -> none  [the longest x1 0.66 us: filter_rows(): hit = (offsets == 2 - n - r)[None, :, None]]
    le x1 -> x0, other arithmetic: 0.73 us -> none  [filter_rows(): keep = jnp.abs(span)[None, :] <= widths[:, None]]
    pallas_call x1, Pallas kernels: 48.3 us -> 48.9 us  [body(): pl.pallas_call(kernel, out_shape=(jax.ShapeDtypeStruct((ROWS, LONS, C), B...]
    unnamed x13 -> x2, local copies, waits for them, and re-layouts: 3.55 us -> 3.39 us
where the time goes in v1:
time: 53.2 us; the launch traced here: 53 us
  Pallas kernels  48.9 us (92%)
  local copies, waits for them, and re-layouts  3.39 us (6%)
  between operations  0.64 us (1%)
    pallas_call x1, Pallas kernels, body(): pl.pallas_call(kernel, out_shape=(jax.ShapeDtypeStruct((ROWS, LONS, C), B...  48.9 us
    unnamed x2, local copies, waits for them, and re-layouts  3.39 us

profile of v1, /device:TPU:1, one launch (start us, length us, event | category | flops | bytes accessed | tf_op | source)
XLA Modules:
  0.0 53.0 jit_solution(1182022541058510580)
XLA Ops:
  0.6 48.9 %sphere_backward.1 = (bf16[4,256,256]{2,1,0:T(8,128)(2,1)}, f32[72,256]{1,0:T(8,128)}) custom-call(bf16[4,256,256]{2,1,0:T(8,128)(2,1)} %g_hbm.1, bf16[4,256,256]{2,1,0:T(8,128)(2,1)} %x_hbm.1, bf16[2304,256]{1,0:T(8,128)(2,1)} %w_hbm.1, bf16[9,3,4,33]{3,2,1,0:T(4,128)(2,1)} %bitcast.3, bf16[9,3,4,2048]{3,2,1,0:T(4,128)(2,1)} %bitcast.2, s32[4]{0:T(128)} %width_ref.1, ...), custom_call_target="tpu_custom_call" | custom-call | tf_op jit(solution)/shard_map/sphere_backward/pallas_call | solution.py:551
  49.6 1.9 %copy.12 = bf16[4,256,256]{2,1,0:T(8,128)(2,1)} copy(bf16[4,256,256]{2,1,0:T(8,128)(2,1)} %get-tuple-element.4) | data formatting | bytes 1048576
  51.4 1.5 %copy.13 = f32[72,256]{1,0:T(8,128)} copy(f32[72,256]{1,0:T(8,128)} %get-tuple-element.5) | data formatting | bytes 147456

commit v2 on v1

--- a/solution.py
+++ b/solution.py
@@ -22,8 +22,10 @@
 DEPTH = 512
 N_LAT = 32
 N_LON = 8
-N_P = 16
+N_Z = 8
 GROUPS = ((0, 3), (3, 6), (6, 9))
+RUNS = ((0, 3, "y"), (3, 6, "x"), (6, 8, "y"), (8, 9, "x"))
+GROUP_RUNS = ((0,), (1,), (2, 3))
 FACTOR = 1.0 / math.sqrt(128 * 2048)
 
 
@@ -33,17 +35,19 @@
 
 def kernel(
     g_hbm, x_hbm, w_hbm, filt_ref, z_hbm, width_ref, offset_ref, polar_ref,
-    ig_hbm, wg_ref,
+    ig_ref, wg_ref,
     gx, xv, xt, wv, wt, lv, vown, vh, vf, tt, hh, zv, zs, yf, yown, yh, yy, ztf, zst, gs_own, gs_buf, gsel,
-    wown, wsnd, cx, s1, rb, s2, pr, s3, fin, igv,
+    wown, wsnd, cx, s1, r1, s2, r2, s3, r3, s4, fin,
     loc_sem, halo_send, halo_recv, vsend, vrecv, ysend, yrecv, gs_send, gs_sem,
-    cs_send, cs_recv, ls_send, ls_recv, ps_send, ps_recv, fs_send, fs_recv, out_sem,
+    cs_send, cs_recv, send1, recv1, send2, recv2, send3, recv3, fs_send, fs_recv,
 ):
     lat = lax.axis_index("lat")
     lon = lax.axis_index("lon")
     core = lax.rem(lat, 2)
-    p = lax.div(lat, 2)
     twin = lat + 1 - 2 * core
+    z, in_plane = lax.div(lat, 4), lax.rem(lat, 4)
+    x_high, x_low, y = lax.div(in_plane, 2), lax.div(lon, 4), lax.rem(lon, 4)
+    place = {"x": 2 * x_high + x_low, "y": y}
 
     def lon_at(step):
         return lax.rem(lon + step, N_LON)
@@ -78,19 +82,24 @@
         pl.semaphore_signal(barrier, inc=1, device_id={"lat": to_lat, "lon": to_lon}, device_id_type=MESH)
 
     outer = lat - 1 + 2 * core
-    has_outer = (outer >= 0) & (outer < N_LAT)
-
-    @pl.when(has_outer)
+    to_next = (core == 1) & (x_high == 1) & (z < N_Z - 1)
+    to_last = (core == 0) & (x_high == 0) & (z > 0)
+    crosses = to_next | to_last
+
+    @pl.when(crosses)
     def _():
         for step in (0, 1, N_LON - 1):
             greet(outer, lon_at(step))
 
-    for step in range(1, N_P):
-        greet(2 * lax.rem(p + step, N_P) + core, lon)
-    for step in range(1, N_LON):
-        greet(lat, lon_at(step))
-    for step in range(N_LON):
-        greet(twin, lon_at(step))
+    def lat_at(step):
+        return 4 * lax.rem(z + step, N_Z) + in_plane
+
+    for step in range(1, N_Z):
+        greet(lat_at(step), lon)
+    for turn_lat in range(4):
+        for step in range(N_LON):
+            if turn_lat or step:
+                greet(4 * z + lax.rem(in_plane + turn_lat, 4), lon_at(step))
 
     span = 2 * REACH + 1
     row_i = lax.broadcasted_iota(jnp.int32, (ROWS, span), 0)
@@ -116,7 +125,7 @@
         placed = placed + dot(lv[n].astype(BF16), where)
     vown[...] = placed.astype(BF16).reshape(8, 16, DEPTH)
 
-    pl.semaphore_wait(barrier, 2 * N_LON + N_P - 2 + 3 * has_outer.astype(jnp.int32))
+    pl.semaphore_wait(barrier, 4 * N_LON + N_Z - 2 + 3 * crosses.astype(jnp.int32))
 
     up, down = lat - 1, lat + 1
     has_up, has_down = lat > 0, lat < N_LAT - 1
@@ -368,92 +377,125 @@
             wsnd[k] = jnp.where(core == 0, second, first).astype(BF16)
         twin_copy(group).start()
 
-    def lon_copy(group, step):
-        k0, k1 = GROUPS[group]
-        to = lon_at(step)
+    def along(axis, step):
+        to = lax.rem(place[axis] + step, 4)
+        if axis == "y":
+            return to, lat, lon + to - y
+        return to, lat + 2 * (lax.div(to, 2) - x_high), lon + 4 * (lax.rem(to, 2) - x_low)
+
+    def first_piece(run, to):
+        k0, k1, axis = RUNS[run]
         at = pl.ds(k0, k1 - k0)
-        src = s1.at[at, pl.ds(pl.multiple_of(32 * to, 32), 32)]
-        return remote(src, rb.at[lon, at], ls_send.at[group, step], ls_recv.at[group], lat, to)
-
-    def over_lon(group):
-        k0, k1 = GROUPS[group]
+        return s1.at[at, to] if axis == "y" else s1.at[at, :, to]
+
+    def first_copy(run, step):
+        k0, k1, axis = RUNS[run]
+        to, to_lat, to_lon = along(axis, step)
+        dst = r1.at[place[axis], pl.ds(k0, k1 - k0)]
+        return remote(first_piece(run, to), dst, send1.at[run, step], recv1.at[run], to_lat, to_lon, "r2")
+
+    def second_copy(run, step):
+        k0, k1, axis = RUNS[run]
+        axis = "x" if axis == "y" else "y"
+        to, to_lat, to_lon = along(axis, step)
         at = pl.ds(k0, k1 - k0)
+        return remote(
+            s2.at[at, to], r2.at[place[axis], at], send2.at[run, step], recv2.at[run], to_lat, to_lon, "r2"
+        )
+
+    def first(group):
         twin_copy(group).wait_recv()
+        for k in range(*GROUPS[group]):
+            s1[k] = (wown[k] + cx[k].astype(F32)).astype(BF16).reshape(4, 4, 16, 128)
+        for run in GROUP_RUNS[group]:
+            for step in range(1, 4):
+                first_copy(run, step).start()
+
+    def arrived(buffer, semaphore):
+        pltpu.make_async_copy(buffer, buffer, semaphore).wait()
+
+    def second(run):
+        k0, k1, axis = RUNS[run]
+        arrived(r1.at[pl.ds(0, 3), pl.ds(k0, k1 - k0)], recv1.at[run])
         for k in range(k0, k1):
-            s1[k] = (wown[k] + cx[k].astype(F32)).astype(BF16)
-        for step in range(1, N_LON):
-            lon_copy(group, step).start()
-        own = s1.at[at, pl.ds(pl.multiple_of(32 * lon, 32), 32)]
-        pltpu.make_async_copy(own, rb.at[lon, at], ls_recv.at[group]).start()
-
-    def granule(k, b):
-        owner = lax.div(16 * k + 2 * lon + b, 9)
+            total = (s1[k, place[axis]] if axis == "y" else s1[k, :, place[axis]]).astype(F32)
+            for step in range(1, 4):
+                total = total + r1[lax.rem(place[axis] + step, 4), k].astype(F32)
+            s2[k] = total.astype(BF16)
+        for step in range(1, 4):
+            second_copy(run, step).start()
+
+    part = 4 * y + place["x"]
+
+    def granule(k):
+        q = 16 * k + part
+        to_z = lax.div(q, 18)
+        b = lax.div(q - 18 * to_z, 16)
         copy = remote(
-            s2.at[k, b], pr.at[b, p], ps_send.at[k, b], ps_recv.at[b], 2 * owner + core, lon
+            s3.at[k], r3.at[b, z], send3.at[k], recv3.at[b], 4 * to_z + in_plane, lon, "r3"
         )
-        return owner, copy
-
-    def over_lat(group):
-        k0, k1 = GROUPS[group]
-        slab = rb.at[:, pl.ds(k0, k1 - k0)]
-        pltpu.make_async_copy(slab, slab, ls_recv.at[group]).wait()
+        return to_z, b, copy
+
+    def third(run):
+        k0, k1, axis = RUNS[run]
+        axis = "x" if axis == "y" else "y"
+        arrived(r2.at[pl.ds(0, 3), pl.ds(k0, k1 - k0)], recv2.at[run])
         for k in range(k0, k1):
-            total = rb[0, k].astype(F32)
-            for step in range(1, N_LON):
-                total = total + rb[step, k].astype(F32)
-            total = total.astype(BF16)
-            for b in range(2):
-                s2[k, b] = total[16 * b:16 * b + 16]
+            total = s2[k, place[axis]].astype(F32)
+            for step in range(1, 4):
+                total = total + r2[lax.rem(place[axis] + step, 4), k].astype(F32)
+            s3[k] = total.astype(BF16)
         for k in range(k0, k1):
-            for b in range(2):
-                owner, copy = granule(k, b)
-
-                @pl.when(owner != p)
-                def _():
-                    copy.start()
-
-                @pl.when(owner == p)
-                def _():
-                    pltpu.make_async_copy(s2.at[k, b], pr.at[b, p], ps_recv.at[b]).start()
-
-    def place(b):
-        k = lax.div(9 * p - 2 * lon - b + 15, 16)
-        e = 16 * k + 2 * lon + b - 9 * p
-        return e, e < 9
-
-    def final_copy(b, e, dc, step):
+            to_z, b, copy = granule(k)
+
+            @pl.when(to_z != z)
+            def _():
+                copy.start()
+
+            @pl.when(to_z == z)
+            def _():
+                pltpu.make_async_copy(s3.at[k], r3.at[b, z], recv3.at[b]).start()
+
+    def owned(b):
+        q = 16 * lax.div(18 * z - part + 15, 16) + part + 16 * b
+        owner = lax.div(q, 9)
+        return q <= 18 * z + 17, owner - 2 * z, q - 9 * owner
+
+    def final_copy(b, to_high, e, dc, step):
         at = pl.ds(pl.multiple_of(16 * e, 16), 16)
-        return remote(
-            s3.at[b], fin.at[core, at], fs_send.at[b, dc, step], fs_recv, twin if dc else lat, lon_at(step)
-        )
+        to_lat = 4 * z + 2 * to_high + (1 - core if dc else core)
+        return remote(s4.at[b], fin.at[core, at], fs_send.at[b, dc, step], fs_recv, to_lat, lon_at(step), "r4")
 
     def needed(e, to_core):
         return ((to_core == 0) & (e <= 4)) | ((to_core == 1) & (e >= 4))
 
     def spread_out():
         for b in range(2):
-            e, valid = place(b)
+            valid, to_high, e = owned(b)
 
             @pl.when(valid)
             def _():
-                pltpu.make_async_copy(pr.at[b], pr.at[b], ps_recv.at[b]).wait()
-                total = pr[b, 0].astype(F32)
-                for step in range(1, N_P):
-                    total = total + pr[b, step].astype(F32)
-                s3[b] = total
+                arrived(r3.at[b], recv3.at[b])
+                total = r3[b, 0].astype(F32)
+                for step in range(1, N_Z):
+                    total = total + r3[b, step].astype(F32)
+                s4[b] = total
 
             for dc in range(2):
                 @pl.when(valid & needed(e, 1 - core if dc else core))
                 def _():
                     for step in range(N_LON):
                         if dc or step:
-                            final_copy(b, e, dc, step).start()
+                            final_copy(b, to_high, e, dc, step).start()
                         else:
-                            at = pl.ds(pl.multiple_of(16 * e, 16), 16)
-                            pltpu.make_async_copy(s3.at[b], fin.at[core, at], fs_recv).start()
-
-    def ig_copy(i2):
-        return pltpu.make_async_copy(igv.at[i2], ig_hbm.at[i2], out_sem.at[i2])
+                            @pl.when(to_high == x_high)
+                            def _():
+                                at = pl.ds(pl.multiple_of(16 * e, 16), 16)
+                                pltpu.make_async_copy(s4.at[b], fin.at[core, at], fs_recv).start()
+
+                            @pl.when(to_high != x_high)
+                            def _():
+                                final_copy(b, to_high, e, 0, 0).start()
 
     circle_total = ztf[...]
     z_high = circle_total.astype(BF16)
@@ -465,23 +507,27 @@
         for a in range(2):
             i2 = 2 * half + a
             twice = jnp.concatenate([yy[i2], yy[i2]], axis=0)
-            igv[i2] = (grad[a * LONS:(a + 1) * LONS] + dot(twice, z_parts, 0, 0)).astype(BF16)
-            ig_copy(i2).start()
+            ig_ref[i2] = (grad[a * LONS:(a + 1) * LONS] + dot(twice, z_parts, 0, 0)).astype(BF16)
 
     spread_rows(far, *GROUPS[0])
     mix(0)
     spread_rows(far, *GROUPS[1])
     mix(1)
-    over_lon(0)
+    first(0)
     spread_rows(far, *GROUPS[2])
     mix(2)
-    over_lon(1)
-    over_lat(0)
-    over_lon(2)
-    over_lat(1)
+    first(1)
+    second(0)
+    first(2)
+    second(1)
+    third(0)
     pull(0)
-    over_lat(2)
+    second(2)
+    second(3)
+    third(1)
     pull(1)
+    third(2)
+    third(3)
     spread_out()
     for index in level:
         halo(index).wait_send()
@@ -515,15 +561,17 @@
 
     for group in range(len(GROUPS)):
         twin_copy(group).wait_send()
-        for step in range(1, N_LON):
-            lon_copy(group, step).wait_send()
+    for run in range(len(RUNS)):
+        for step in range(1, 4):
+            first_copy(run, step).wait_send()
+            second_copy(run, step).wait_send()
     for k in range(K):
-        for b in range(2):
-            owner, copy = granule(k, b)
-
-            @pl.when(owner != p)
-            def _():
-                copy.wait_send()
+        to_z, b, copy = granule(k)
+
+        @pl.when(to_z != z)
+        def _():
+            copy.wait_send()
+
     some = fin.at[:, pl.ds(0, 80)]
     pltpu.make_async_copy(some, some, fs_recv).wait()
     rows = pl.ds(pl.multiple_of(72 * core, 8), 72)
@@ -531,15 +579,17 @@
         wg_ref[:, pl.ds(128 * half, 128)] = fin[half, rows, :]
 
     for b in range(2):
-        e, valid = place(b)
+        valid, to_high, e = owned(b)
         for dc in range(2):
             @pl.when(valid & needed(e, 1 - core if dc else core))
             def _():
                 for step in range(N_LON):
                     if dc or step:
-                        final_copy(b, e, dc, step).wait_send()
-    for i2 in range(ROWS):
-        ig_copy(i2).wait()
+                        final_copy(b, to_high, e, dc, step).wait_send()
+                    else:
+                        @pl.when(to_high != x_high)
+                        def _():
+                            final_copy(b, to_high, e, 0, 0).wait_send()
 
 
 def body(input_field, grad_out, weight, filt, zonal_weight, widths, offsets, polar_rows):
@@ -547,15 +597,12 @@
     hbm = pl.BlockSpec(memory_space=pltpu.HBM)
     vmem = pl.BlockSpec(memory_space=pltpu.VMEM)
     smem = pl.BlockSpec(memory_space=pltpu.SMEM)
-    groups = len(GROUPS)
+    groups, runs = len(GROUPS), len(RUNS)
     return pl.pallas_call(
         kernel,
-        out_shape=(
-            jax.ShapeDtypeStruct((ROWS, LONS, C), BF16),
-            jax.ShapeDtypeStruct((72, C), F32),
-        ),
+        out_shape=(pltpu.VMEM((ROWS, LONS, C), BF16), pltpu.VMEM((72, C), F32)),
         in_specs=[hbm, hbm, hbm, vmem, hbm, smem, smem, smem],
-        out_specs=(pl.BlockSpec(memory_space=pl.ANY), vmem),
+        out_specs=(vmem, vmem),
         scratch_shapes=[
             pltpu.VMEM((8, LONS + 2 * REACH, C), BF16),
             pltpu.VMEM((ROWS, LONS, C), BF16),
@@ -582,25 +629,29 @@
             pltpu.VMEM((K, C, 128), F32),
             pltpu.VMEM((K, C, 128), BF16),
             pltpu.VMEM((K, C, 128), BF16),
-            pltpu.VMEM((K, C, 128), BF16),
-            pltpu.VMEM((N_LON, K, 32, 128), BF16),
-            pltpu.VMEM((K, 2, 16, 128), BF16),
-            pltpu.VMEM((2, N_P, 16, 128), BF16),
+            pltpu.VMEM((K, 4, 4, 16, 128), BF16),
+            pltpu.VMEM((4, K, 4, 16, 128), BF16),
+            pltpu.VMEM((K, 4, 16, 128), BF16),
+            pltpu.VMEM((4, K, 16, 128), BF16),
+            pltpu.VMEM((K, 16, 128), BF16),
+            pltpu.VMEM((2, N_Z, 16, 128), BF16),
             pltpu.VMEM((2, 16, 128), F32),
             pltpu.VMEM((2, 144, 128), F32),
-            pltpu.VMEM((ROWS, LONS, C), BF16),
             dma((4,)), dma((8,)), dma((8,)), dma((2,)), dma((2,)), dma, dma, dma((2, N_LON)), dma,
-            dma((groups,)), dma((groups,)), dma((groups, N_LON)), dma((groups,)),
-            dma((K, 2)), dma((2,)), dma((2, 2, N_LON)), dma, dma((ROWS,)),
+            dma((groups,)), dma((groups,)), dma((runs, 4)), dma((runs,)), dma((runs, 4)), dma((runs,)),
+            dma((K,)), dma((2,)), dma((2, 2, N_LON)), dma,
         ],
         compiler_params=pltpu.CompilerParams(
-            collective_id=0, has_side_effects=True, vmem_limit_bytes=60 * 1024 * 1024
+            collective_id=0, has_side_effects=True, vmem_limit_bytes=48 * 1024 * 1024
         ),
         name="sphere_backward",
-    )(
-        grad_out, input_field, weight, jnp.transpose(filt, (0, 2, 1, 3)),
-        jnp.transpose(zonal_weight, (0, 2, 1, 3)), widths, offsets, polar_rows,
-    )
+    )(*[
+        pltpu.with_memory_space_constraint(array, pltpu.HBM)
+        for array in (
+            grad_out, input_field, weight, jnp.transpose(filt, (0, 2, 1, 3)),
+            jnp.transpose(zonal_weight, (0, 2, 1, 3)), widths, offsets, polar_rows,
+        )
+    ])
 
 
 def solution(mesh):

time: 53.2 us -> 50.5 us (0.949)
  local copies, waits for them, and re-layouts: 3.39 us -> 1.43 us
  Pallas kernels: 48.9 us -> 48.2 us
    unnamed x2, local copies, waits for them, and re-layouts: 3.39 us -> 1.43 us
    pallas_call x1, Pallas kernels: 48.9 us -> 48.2 us  [body(): pl.pallas_call(kernel, out_shape=(pltpu.VMEM((ROWS, LONS, C), BF16), pltp...]
where the time goes in v2:
time: 50.5 us; the launch traced here: 50.2 us
  Pallas kernels  48.2 us (95%)
  local copies, waits for them, and re-layouts  1.43 us (3%)
  between operations  0.64 us (1%)
    pallas_call x1, Pallas kernels, body(): pl.pallas_call(kernel, out_shape=(pltpu.VMEM((ROWS, LONS, C), BF16), pltp...  48.2 us
    unnamed x2, local copies, waits for them, and re-layouts  1.43 us

profile of v2, /device:TPU:1, one launch (start us, length us, event | category | flops | bytes accessed | tf_op | source)
XLA Modules:
  0.0 50.2 jit_solution(286109869062393057)
XLA Ops:
  0.6 48.2 %sphere_backward.1 = (bf16[4,256,256]{2,1,0:T(8,128)(2,1)S(1)}, f32[72,256]{1,0:T(8,128)S(1)}) custom-call(bf16[4,256,256]{2,1,0:T(8,128)(2,1)} %g_hbm.1, bf16[4,256,256]{2,1,0:T(8,128)(2,1)} %x_hbm.1, bf16[2304,256]{1,0:T(8,128)(2,1)} %w_hbm.1, bf16[9,3,4,33]{3,2,1,0:T(4,128)(2,1)} %bitcast.3, bf16[9,3,4,2048]{3,2,1,0:T(4,128)(2,1)} %bitcast.2, ...), custom_call_target="tpu_custom_call" | custom-call | tf_op jit(solution)/shard_map/sphere_backward/pallas_call | solution.py:601
  48.8 0.8 %copy.12 = bf16[4,256,256]{2,1,0:T(8,128)(2,1)} copy(bf16[4,256,256]{2,1,0:T(8,128)(2,1)S(1)} %get-tuple-element.2) | data formatting | bytes 1048576
  49.6 0.6 %copy.13 = f32[72,256]{1,0:T(8,128)} copy(f32[72,256]{1,0:T(8,128)S(1)} %get-tuple-element.3) | data formatting | bytes 147456

commit v3 on v2

--- a/solution.py
+++ b/solution.py
@@ -151,20 +151,28 @@
         src = vown.at[pl.ds(6, 2)] if side == 0 else vown.at[pl.ds(0, 2)]
         return remote(src, vh.at[side], vsend.at[side], vrecv.at[side], down if side == 0 else up, lon, "halo")
 
-    @pl.when(has_down)
-    def _():
-        v_halo(0).start()
-        for index in from_up:
-            halo(index).start()
-
-    @pl.when(has_up)
-    def _():
-        v_halo(1).start()
-        for index in from_down:
-            halo(index).start()
-
     for index in level:
         halo(index).start()
+
+    @pl.when(has_down)
+    def _():
+        v_halo(0).start()
+        for index in from_up[1:]:
+            halo(index).start()
+
+    @pl.when(has_up)
+    def _():
+        v_halo(1).start()
+        for index in from_down[1:]:
+            halo(index).start()
+
+    @pl.when(has_down)
+    def _():
+        halo(from_up[0]).start()
+
+    @pl.when(has_up)
+    def _():
+        halo(from_down[0]).start()
 
     g_copy.wait()
 
@@ -259,12 +267,11 @@
 
         lax.fori_loop(0, K, band, 0)
 
-    def spread_rows(base, k0, k1):
+    def spread_rows(base, k0, k1, blocks):
         def spread(step, carry):
-            for half in range(2):
-                index = 2 * step + half
-                i2, jb = base + lax.div(index, LONS // JB), lax.rem(index, LONS // JB)
-                at = pl.ds(pl.multiple_of(jb * JB, JB), WIN)
+            for jb in blocks:
+                i2 = base + step
+                at = pl.ds(jb * JB, WIN)
                 windows = [gx[i2 + n, at, :] for n in range(CANDS)]
                 windows.append(jnp.zeros((DEPTH - CANDS * WIN, C), BF16))
                 moved = dot(tt[i2, pl.ds(k0 * JB, (k1 - k0) * JB)], jnp.concatenate(windows, axis=0)).astype(BF16)
@@ -273,7 +280,7 @@
                     hh[rows, pl.ds(k * C, C)] = moved[(k - k0) * JB:(k - k0 + 1) * JB]
             return carry
 
-        lax.fori_loop(0, LONS // JB, spread, 0)
+        lax.fori_loop(0, 2, spread, 0)
 
     near, far = 2 - 2 * core, 2 * core
 
@@ -281,20 +288,18 @@
         for index in index_list:
             halo(index).wait_recv()
 
-    arrive(level)
-
     @pl.when(core == 0)
     def _():
         v_halo(1).wait_recv()
-        arrive(from_down)
+        arrive(from_down[:1])
 
     @pl.when(core == 1)
     def _():
         v_halo(0).wait_recv()
-        arrive(from_up)
+        arrive(from_up[:1])
 
     band_rows(near, 1 - core)
-    spread_rows(near, 0, K)
+    spread_rows(near, 0, K, (1, 2))
 
     @pl.when((core == 0) & has_up)
     def _():
@@ -354,6 +359,18 @@
         for q in range(2):
             ztf[pl.ds(16 * q + k, 1), :] = mixed[q:q + 1]
 
+    arrive(level)
+
+    @pl.when(core == 0)
+    def _():
+        arrive(from_down[1:])
+
+    @pl.when(core == 1)
+    def _():
+        arrive(from_up[1:])
+
+    spread_rows(near, 0, K, (0, 3))
+
     @pl.when((core == 0) & has_up)
     def _():
         arrive(from_up)
@@ -509,23 +526,23 @@
             twice = jnp.concatenate([yy[i2], yy[i2]], axis=0)
             ig_ref[i2] = (grad[a * LONS:(a + 1) * LONS] + dot(twice, z_parts, 0, 0)).astype(BF16)
 
-    spread_rows(far, *GROUPS[0])
+    spread_rows(far, *GROUPS[0], range(4))
     mix(0)
-    spread_rows(far, *GROUPS[1])
+    spread_rows(far, *GROUPS[1], range(4))
     mix(1)
     first(0)
-    spread_rows(far, *GROUPS[2])
+    spread_rows(far, *GROUPS[2], range(4))
     mix(2)
     first(1)
+    first(2)
     second(0)
-    first(2)
     second(1)
+    pull(0)
     third(0)
-    pull(0)
     second(2)
     second(3)
+    pull(1)
     third(1)
-    pull(1)
     third(2)
     third(3)
     spread_out()

time: 50.5 us -> 45.4 us (0.90)
  Pallas kernels: 48.2 us -> 43.2 us
    pallas_call x1, Pallas kernels: 48.2 us -> 43.2 us  [body(): pl.pallas_call(kernel, out_shape=(pltpu.VMEM((ROWS, LONS, C), BF16), pltp...]
where the time goes in v3:
time: 45.4 us; the launch traced here: 45.3 us
  Pallas kernels  43.2 us (95%)
  local copies, waits for them, and re-layouts  1.43 us (3%)
  between operations  0.64 us (1%)
    pallas_call x1, Pallas kernels, body(): pl.pallas_call(kernel, out_shape=(pltpu.VMEM((ROWS, LONS, C), BF16), pltp...  43.2 us
    unnamed x2, local copies, waits for them, and re-layouts  1.43 us

profile of v3, /device:TPU:1, one launch (start us, length us, event | category | flops | bytes accessed | tf_op | source)
XLA Modules:
  0.0 45.3 jit_solution(12246207360513676603)
XLA Ops:
  0.6 43.2 %sphere_backward.1 = (bf16[4,256,256]{2,1,0:T(8,128)(2,1)S(1)}, f32[72,256]{1,0:T(8,128)S(1)}) custom-call(bf16[4,256,256]{2,1,0:T(8,128)(2,1)} %g_hbm.1, bf16[4,256,256]{2,1,0:T(8,128)(2,1)} %x_hbm.1, bf16[2304,256]{1,0:T(8,128)(2,1)} %w_hbm.1, bf16[9,3,4,33]{3,2,1,0:T(4,128)(2,1)} %bitcast.3, bf16[9,3,4,2048]{3,2,1,0:T(4,128)(2,1)} %bitcast.2, ...), custom_call_target="tpu_custom_call" | custom-call | tf_op jit(solution)/shard_map/sphere_backward/pallas_call | solution.py:618
  43.8 0.8 %copy.12 = bf16[4,256,256]{2,1,0:T(8,128)(2,1)} copy(bf16[4,256,256]{2,1,0:T(8,128)(2,1)S(1)} %get-tuple-element.2) | data formatting | bytes 1048576
  44.6 0.6 %copy.13 = f32[72,256]{1,0:T(8,128)} copy(f32[72,256]{1,0:T(8,128)S(1)} %get-tuple-element.3) | data formatting | bytes 147456

commit v4 on v2

--- a/solution.py
+++ b/solution.py
@@ -23,9 +23,9 @@
 N_LAT = 32
 N_LON = 8
 N_Z = 8
-GROUPS = ((0, 3), (3, 6), (6, 9))
-RUNS = ((0, 3, "y"), (3, 6, "x"), (6, 8, "y"), (8, 9, "x"))
-GROUP_RUNS = ((0,), (1,), (2, 3))
+GROUPS = ((0, 4), (4, 7), (7, 9))
+RUNS = ((0, 2, "y"), (2, 4, "x"), (4, 6, "x"), (6, 7, "y"), (7, 8, "y"), (8, 9, "x"))
+GROUP_RUNS = ((0, 1), (2, 3), (4, 5))
 FACTOR = 1.0 / math.sqrt(128 * 2048)
 
 
@@ -34,9 +34,10 @@
 
 
 def kernel(
-    g_hbm, x_hbm, w_hbm, filt_ref, z_hbm, width_ref, offset_ref, polar_ref,
+    g_hbm, x_hbm, w_hbm, filt_hbm, z_hbm, width_hbm, offset_hbm, polar_hbm,
     ig_ref, wg_ref,
-    gx, xv, xt, wv, wt, lv, vown, vh, vf, tt, hh, zv, zs, yf, yown, yh, yy, ztf, zst, gs_own, gs_buf, gsel,
+    filt_ref, width_ref, offset_ref, polar_ref,
+    gx, gfar, xv, xt, wv, wt, lv, vown, vtwin, vfar, vf, vfh, tt, tth, facc, hh, wnear, zv, zs, yf, yown, yh, yy, ztf, zparts, zst, gs_own, gs_buf, gsel,
     wown, wsnd, cx, s1, r1, s2, r2, s3, r3, s4, fin,
     loc_sem, halo_send, halo_recv, vsend, vrecv, ysend, yrecv, gs_send, gs_sem,
     cs_send, cs_recv, send1, recv1, send2, recv2, send3, recv3, fs_send, fs_recv,
@@ -62,12 +63,45 @@
     polar_dev = north | south
     affected = polar_dev | (lat == 1) | (lat == N_LAT - 2)
 
+    barrier = pltpu.get_barrier_semaphore()
+
+    def greet(to_lat, to_lon):
+        pl.semaphore_signal(barrier, inc=1, device_id={"lat": to_lat, "lon": to_lon}, device_id_type=MESH)
+
+    outer = lat - 1 + 2 * core
+    to_next = (core == 1) & (x_high == 1) & (z < N_Z - 1)
+    to_last = (core == 0) & (x_high == 0) & (z > 0)
+    crosses = to_next | to_last
+
+    @pl.when(crosses)
+    def _():
+        for step in (0, 1, N_LON - 1):
+            greet(outer, lon_at(step))
+
+    def lat_at(step):
+        return 4 * lax.rem(z + step, N_Z) + in_plane
+
+    for step in range(1, N_Z):
+        greet(lat_at(step), lon)
+    for turn_lat in range(4):
+        for step in range(N_LON):
+            if turn_lat or step:
+                greet(4 * z + lax.rem(in_plane + turn_lat, 4), lon_at(step))
+
     g_copy = pltpu.make_async_copy(g_hbm, gx.at[pl.ds(2, ROWS), pl.ds(REACH, LONS)], loc_sem.at[0])
     x_copy = pltpu.make_async_copy(x_hbm, xv, loc_sem.at[1])
     w_copy = pltpu.make_async_copy(w_hbm, wv, loc_sem.at[2])
     z_copy = pltpu.make_async_copy(
         z_hbm.at[:, :, :, pl.ds(pl.multiple_of(lon * LONS, LONS), LONS)], zv, loc_sem.at[3]
     )
+    small = [
+        pltpu.make_async_copy(src, dst, loc_sem.at[4 + index])
+        for index, (src, dst) in enumerate(
+            ((filt_hbm, filt_ref), (width_hbm, width_ref), (offset_hbm, offset_ref), (polar_hbm, polar_ref))
+        )
+    ]
+    for copy in small:
+        copy.start()
     g_copy.start()
     x_copy.start()
     w_copy.start()
@@ -76,31 +110,8 @@
     def _():
         z_copy.start()
 
-    barrier = pltpu.get_barrier_semaphore()
-
-    def greet(to_lat, to_lon):
-        pl.semaphore_signal(barrier, inc=1, device_id={"lat": to_lat, "lon": to_lon}, device_id_type=MESH)
-
-    outer = lat - 1 + 2 * core
-    to_next = (core == 1) & (x_high == 1) & (z < N_Z - 1)
-    to_last = (core == 0) & (x_high == 0) & (z > 0)
-    crosses = to_next | to_last
-
-    @pl.when(crosses)
-    def _():
-        for step in (0, 1, N_LON - 1):
-            greet(outer, lon_at(step))
-
-    def lat_at(step):
-        return 4 * lax.rem(z + step, N_Z) + in_plane
-
-    for step in range(1, N_Z):
-        greet(lat_at(step), lon)
-    for turn_lat in range(4):
-        for step in range(N_LON):
-            if turn_lat or step:
-                greet(4 * z + lax.rem(in_plane + turn_lat, 4), lon_at(step))
-
+    for copy in small:
+        copy.wait()
     span = 2 * REACH + 1
     row_i = lax.broadcasted_iota(jnp.int32, (ROWS, span), 0)
     tap = lax.broadcasted_iota(jnp.int32, (ROWS, span), 1)
@@ -125,48 +136,67 @@
         placed = placed + dot(lv[n].astype(BF16), where)
     vown[...] = placed.astype(BF16).reshape(8, 16, DEPTH)
 
+    g_copy.wait()
     pl.semaphore_wait(barrier, 4 * N_LON + N_Z - 2 + 3 * crosses.astype(jnp.int32))
 
-    up, down = lat - 1, lat + 1
-    has_up, has_down = lat > 0, lat < N_LAT - 1
-    rows_of = {-1: (0, 2, 6), 0: (0, ROWS, 2), 1: (2, 2, 0)}
+    has_far = (outer >= 0) & (outer < N_LAT)
+    near, far = 2 - 2 * core, 2 * core
     cols_of = {-1: (0, REACH, REACH + LONS), 0: (0, LONS, REACH), 1: (LONS - REACH, REACH, 0)}
-    moves = [(1, 0), (-1, 0), (1, 1), (1, -1), (-1, 1), (-1, -1), (0, 1), (0, -1)]
-    from_up = [index for index in range(8) if moves[index][0] == 1]
-    from_down = [index for index in range(8) if moves[index][0] == -1]
-    level = [index for index in range(8) if moves[index][0] == 0]
-
-    def halo(index):
-        dlat, dlon = moves[index]
-        r0, rn, r_to = rows_of[dlat]
+    level, to_twin, to_far = ((0, 1), (1, -1)), ((2, 0), (3, 1), (4, -1)), ((5, 0), (6, 1), (7, -1))
+
+    def halo(kind, index, dlon):
         c0, cn, c_to = cols_of[dlon]
+        cols, to_cols = pl.ds(REACH + c0, cn), pl.ds(c_to, cn)
+        if kind == "level":
+            src, dst, to_lat = gx.at[pl.ds(2, ROWS), cols], gx.at[pl.ds(2, ROWS), to_cols], lat
+        elif kind == "twin":
+            src, dst, to_lat = gx.at[pl.ds(2 + near, 2), cols], gx.at[pl.ds(6 * core, 2), to_cols], twin
+        else:
+            src, dst, to_lat = gx.at[pl.ds(2 + far, 2), cols], gfar.at[:, to_cols], outer
         return remote(
-            g_hbm.at[pl.ds(r0, rn), pl.ds(c0, cn)],
-            gx.at[pl.ds(r_to, rn), pl.ds(c_to, cn)],
-            halo_send.at[index], halo_recv.at[index],
-            lat + dlat, lon_at(dlon % N_LON), "halo",
+            src, dst, halo_send.at[index], halo_recv.at[index], to_lat, lon_at(dlon % N_LON),
+            "big" if kind == "far" and dlon == 0 else "halo",
         )
 
-    def v_halo(side):
-        src = vown.at[pl.ds(6, 2)] if side == 0 else vown.at[pl.ds(0, 2)]
-        return remote(src, vh.at[side], vsend.at[side], vrecv.at[side], down if side == 0 else up, lon, "halo")
-
-    @pl.when(has_down)
-    def _():
-        v_halo(0).start()
-        for index in from_up:
-            halo(index).start()
-
-    @pl.when(has_up)
-    def _():
-        v_halo(1).start()
-        for index in from_down:
-            halo(index).start()
-
-    for index in level:
-        halo(index).start()
-
-    g_copy.wait()
+    def arrived(buffer, semaphore):
+        pltpu.make_async_copy(buffer, buffer, semaphore).wait()
+
+    def arrive(kind, moves):
+        for index, dlon in moves:
+            c0, cn, c_to = cols_of[dlon]
+            cols = pl.ds(c_to, cn)
+            if kind == "level":
+                place_of = gx.at[pl.ds(2, ROWS), cols]
+            elif kind == "twin":
+                place_of = gx.at[pl.ds(6 - 6 * core, 2), cols]
+            else:
+                place_of = gfar.at[:, cols]
+            arrived(place_of, halo_recv.at[index])
+
+    def v_twin():
+        return remote(vown.at[pl.ds(6 - 6 * core, 2)], vtwin, vsend.at[0], vrecv.at[0], twin, lon, "halo")
+
+    def v_far():
+        return remote(vown.at[pl.ds(6 * core, 2)], vfar, vsend.at[1], vrecv.at[1], outer, lon, "halo")
+
+    for move in level:
+        halo("level", *move).start()
+    v_twin().start()
+    for move in to_twin:
+        halo("twin", *move).start()
+
+    @pl.when(has_far)
+    def _():
+        v_far().start()
+        for move in to_far[1:] + to_far[:1]:
+            halo("far", *move).start()
+
+    gx[pl.ds(6 * core, 2)] = jnp.zeros((2,) + gx.shape[1:], BF16)
+
+    @pl.when(jnp.logical_not(has_far))
+    def _():
+        gfar[...] = jnp.zeros_like(gfar)
+        vfar[...] = jnp.zeros_like(vfar)
 
     def gs_copy(dc, step):
         return remote(
@@ -224,87 +254,69 @@
     def _():
         y_halo(0).start()
 
-    @pl.when(north)
-    def _():
-        gx[pl.ds(0, 2)] = jnp.zeros((2,) + gx.shape[1:], BF16)
-        vh[0] = jnp.zeros(vh.shape[1:], BF16)
-
-    @pl.when(south)
-    def _():
-        gx[pl.ds(6, 2)] = jnp.zeros((2,) + gx.shape[1:], BF16)
-        vh[1] = jnp.zeros(vh.shape[1:], BF16)
-
     x_copy.wait()
     for i in range(ROWS):
         xt[:, pl.ds(i * LONS, LONS)] = xv[i].T
-    w_copy.wait()
-
-    def turn(k, carry):
-        at = pl.ds(pl.multiple_of(k * C, C), C)
-        wt[at, :] = wv[at, :].T
-        return carry
-
-    lax.fori_loop(0, K, turn, 0)
-
-    def band_rows(base, side):
-        for a in range(2):
-            vf[pl.ds(16 * a, 16), :] = vown[2 + base + a].astype(F32) + vh[side, a].astype(F32)
-
-        def band(k, carry):
-            for a in range(2):
-                row = jnp.broadcast_to(vf[pl.ds(16 * a + k, 1), :], (JB, DEPTH))
-                rolled = pltpu.roll(row, 0, 1, stride=1, stride_axis=0)
-                tt[base + a, pl.ds(pl.multiple_of(k * JB, JB), JB), :] = rolled.astype(BF16)
+    def band_rows(rows, lanes, put):
+        def band(step, carry):
+            for k in (3 * step, 3 * step + 1, 3 * step + 2):
+                for a in range(2):
+                    row = jnp.broadcast_to(rows[pl.ds(16 * a + k, 1), :], (JB, lanes))
+                    rolled = pltpu.roll(row, 0, 1, stride=1, stride_axis=0)
+                    put(a)[pl.ds(pl.multiple_of(k * JB, JB), JB), :] = rolled.astype(BF16)
             return carry
 
-        lax.fori_loop(0, K, band, 0)
-
-    def spread_rows(base, k0, k1):
+        lax.fori_loop(0, K // 3, band, 0)
+
+    def own_windows(i2, jb):
+        windows = [gx[i2 + n, pl.ds(jb * JB, WIN), :] for n in range(CANDS)]
+        windows.append(jnp.zeros((DEPTH - CANDS * WIN, C), BF16))
+        return jnp.concatenate(windows, axis=0)
+
+    def put_rows(i2, jb, k0, k1, moved):
+        rows = pl.ds(pl.multiple_of(i2 * LONS + jb * JB, JB), JB)
+        for k in range(k0, k1):
+            hh[rows, pl.ds(k * C, C)] = moved[(k - k0) * JB:(k - k0 + 1) * JB]
+
+    def spread_near(blocks):
         def spread(step, carry):
-            for half in range(2):
-                index = 2 * step + half
-                i2, jb = base + lax.div(index, LONS // JB), lax.rem(index, LONS // JB)
-                at = pl.ds(pl.multiple_of(jb * JB, JB), WIN)
-                windows = [gx[i2 + n, at, :] for n in range(CANDS)]
-                windows.append(jnp.zeros((DEPTH - CANDS * WIN, C), BF16))
-                moved = dot(tt[i2, pl.ds(k0 * JB, (k1 - k0) * JB)], jnp.concatenate(windows, axis=0)).astype(BF16)
-                rows = pl.ds(pl.multiple_of(i2 * LONS + jb * JB, JB), JB)
-                for k in range(k0, k1):
-                    hh[rows, pl.ds(k * C, C)] = moved[(k - k0) * JB:(k - k0 + 1) * JB]
+            for jb in blocks:
+                i2 = near + step
+                put_rows(i2, jb, 0, K, dot(tt[i2], own_windows(i2, jb)).astype(BF16))
             return carry
 
-        lax.fori_loop(0, LONS // JB, spread, 0)
-
-    near, far = 2 - 2 * core, 2 * core
-
-    def arrive(index_list):
-        for index in index_list:
-            halo(index).wait_recv()
-
-    arrive(level)
-
-    @pl.when(core == 0)
-    def _():
-        v_halo(1).wait_recv()
-        arrive(from_down)
-
-    @pl.when(core == 1)
-    def _():
-        v_halo(0).wait_recv()
-        arrive(from_up)
-
-    band_rows(near, 1 - core)
-    spread_rows(near, 0, K)
-
-    @pl.when((core == 0) & has_up)
-    def _():
-        v_halo(0).wait_recv()
-
-    @pl.when((core == 1) & has_down)
-    def _():
-        v_halo(1).wait_recv()
-
-    band_rows(far, core)
+        lax.fori_loop(0, 2, spread, 0)
+
+    def spread_far_own():
+        def spread(step, carry):
+            for jb in range(4):
+                facc[4 * step + jb] = dot(tt[far + step], own_windows(far + step, jb))
+            return carry
+
+        lax.fori_loop(0, 2, spread, 0)
+
+    def spread_far(k0, k1):
+        at = pl.ds(k0 * JB, (k1 - k0) * JB)
+
+        def spread(step, carry):
+            for jb in range(4):
+                windows = [gfar[n, pl.ds(jb * JB, WIN), :] for n in range(2)]
+                windows.append(jnp.zeros((256 - 2 * WIN, C), BF16))
+                moved = facc[4 * step + jb, at] + dot(tth[step, at], jnp.concatenate(windows, axis=0))
+                put_rows(far + step, jb, k0, k1, moved.astype(BF16))
+            return carry
+
+        lax.fori_loop(0, 2, spread, 0)
+
+    v_twin().wait_recv()
+    arrive("twin", to_twin[:1])
+    for a in range(2):
+        vf[pl.ds(16 * a, 16), :] = vown[2 + near + a].astype(F32) + vtwin[a].astype(F32)
+    band_rows(vf, DEPTH, lambda a: tt.at[near + a])
+    spread_near((1, 2))
+    for a in range(2):
+        vf[pl.ds(16 * a, 16), :] = vown[2 + far + a].astype(F32)
+    band_rows(vf, DEPTH, lambda a: tt.at[far + a])
 
     for i2 in range(ROWS):
         yy[i2] = yown[2 + i2]
@@ -343,24 +355,32 @@
                 picked = picked + total[i:i + 1] * (mine == i).astype(F32)
             gsel[pl.ds(q, 1), :] = picked
 
-    circle_sum = gsel[...]
-    high = circle_sum.astype(BF16)
-    low = (circle_sum - high.astype(F32)).astype(BF16)
-    parts = jnp.concatenate([high.astype(F32), low.astype(F32)], axis=0).astype(BF16)
-    ztf[...] = jnp.zeros_like(ztf)
+    arrive("level", level)
+    arrive("twin", to_twin[1:])
+    spread_near((0, 3))
+    spread_far_own()
+    near_lons = pl.ds(pl.multiple_of(near * LONS, 2 * LONS), 2 * LONS)
+    far_lons = pl.ds(pl.multiple_of(far * LONS, 2 * LONS), 2 * LONS)
     for k in range(K):
-        mixed = dot(parts, wt[pl.ds(k * C, C), :])
-        mixed = mixed[:8] + mixed[8:]
+        share = dot(xt[:, near_lons], hh[near_lons, pl.ds(k * C, C)]) * FACTOR
         for q in range(2):
-            ztf[pl.ds(16 * q + k, 1), :] = mixed[q:q + 1]
-
-    @pl.when((core == 0) & has_up)
-    def _():
-        arrive(from_up)
-
-    @pl.when((core == 1) & has_down)
-    def _():
-        arrive(from_down)
+            share = share + zst[:, 16 * q + k:16 * q + k + 1] * gsel[q:q + 1, :]
+        wnear[k] = share
+
+    @pl.when(has_far)
+    def _():
+        arrived(vfar, vrecv.at[1])
+
+    for a in range(2):
+        values = vfar[a].astype(F32)
+        low_side = pltpu.roll(values, WIN * a, 1) if a else values
+        high_side = pltpu.roll(values, 128 + WIN * a, 1)
+        vfh[pl.ds(16 * a, 16), :] = jnp.where(core == 0, low_side, high_side)[:, :256]
+    band_rows(vfh, 256, lambda a: tth.at[a])
+
+    @pl.when(has_far)
+    def _():
+        arrive("far", to_far)
 
     def twin_copy(group):
         k0, k1 = GROUPS[group]
@@ -369,9 +389,7 @@
 
     def mix(group):
         for k in range(*GROUPS[group]):
-            share = dot(xt[...], hh[:, pl.ds(k * C, C)]) * FACTOR
-            for q in range(2):
-                share = share + zst[:, 16 * q + k:16 * q + k + 1] * gsel[q:q + 1, :]
+            share = wnear[k] + dot(xt[:, far_lons], hh[far_lons, pl.ds(k * C, C)]) * FACTOR
             first, second = share[:, :128], share[:, 128:]
             wown[k] = jnp.where(core == 0, first, second)
             wsnd[k] = jnp.where(core == 0, second, first).astype(BF16)
@@ -410,9 +428,6 @@
         for run in GROUP_RUNS[group]:
             for step in range(1, 4):
                 first_copy(run, step).start()
-
-    def arrived(buffer, semaphore):
-        pltpu.make_async_copy(buffer, buffer, semaphore).wait()
 
     def second(run):
         k0, k1, axis = RUNS[run]
@@ -497,52 +512,77 @@
                             def _():
                                 final_copy(b, to_high, e, 0, 0).start()
 
-    circle_total = ztf[...]
-    z_high = circle_total.astype(BF16)
-    z_low = (circle_total - z_high.astype(F32)).astype(BF16)
-    z_parts = jnp.concatenate([z_high, z_low], axis=0)
+    def prepare_pull():
+        w_copy.wait()
+
+        def turn(k, carry):
+            at = pl.ds(pl.multiple_of(k * C, C), C)
+            wt[at, :] = wv[at, :].T
+            return carry
+
+        lax.fori_loop(0, K, turn, 0)
+
+        circle_sum = gsel[...]
+        high = circle_sum.astype(BF16)
+        low = (circle_sum - high.astype(F32)).astype(BF16)
+        parts = jnp.concatenate([high.astype(F32), low.astype(F32)], axis=0).astype(BF16)
+        ztf[...] = jnp.zeros_like(ztf)
+        for k in range(K):
+            mixed = dot(parts, wt[pl.ds(k * C, C), :])
+            mixed = mixed[:8] + mixed[8:]
+            for q in range(2):
+                ztf[pl.ds(16 * q + k, 1), :] = mixed[q:q + 1]
+
+        circle_total = ztf[...]
+        z_high = circle_total.astype(BF16)
+        z_low = (circle_total - z_high.astype(F32)).astype(BF16)
+        z_parts = jnp.concatenate([z_high, z_low], axis=0)
+        zparts[...] = z_parts
 
     def pull(half):
+        z_parts = zparts[...]
         grad = dot(hh[pl.ds(half * 2 * LONS, 2 * LONS), :], wt[...])
         for a in range(2):
             i2 = 2 * half + a
             twice = jnp.concatenate([yy[i2], yy[i2]], axis=0)
             ig_ref[i2] = (grad[a * LONS:(a + 1) * LONS] + dot(twice, z_parts, 0, 0)).astype(BF16)
 
-    spread_rows(far, *GROUPS[0])
+    spread_far(*GROUPS[0])
     mix(0)
-    spread_rows(far, *GROUPS[1])
+    spread_far(*GROUPS[1])
     mix(1)
     first(0)
-    spread_rows(far, *GROUPS[2])
+    spread_far(*GROUPS[2])
     mix(2)
     first(1)
+    first(2)
     second(0)
-    first(2)
     second(1)
-    third(0)
+    prepare_pull()
     pull(0)
     second(2)
     second(3)
+    third(0)
     third(1)
+    second(4)
+    second(5)
     pull(1)
     third(2)
     third(3)
+    third(4)
+    third(5)
     spread_out()
-    for index in level:
-        halo(index).wait_send()
-
-    @pl.when(has_down)
-    def _():
-        v_halo(0).wait_send()
-        for index in from_up:
-            halo(index).wait_send()
-
-    @pl.when(has_up)
-    def _():
-        v_halo(1).wait_send()
-        for index in from_down:
-            halo(index).wait_send()
+    for move in level:
+        halo("level", *move).wait_send()
+    v_twin().wait_send()
+    for move in to_twin:
+        halo("twin", *move).wait_send()
+
+    @pl.when(has_far)
+    def _():
+        v_far().wait_send()
+        for move in to_far:
+            halo("far", *move).wait_send()
 
     @pl.when(north)
     def _():
@@ -592,29 +632,47 @@
                             final_copy(b, to_high, e, 0, 0).wait_send()
 
 
+def store(ig_ref, wg_ref, ig_hbm, wg_hbm, sem):
+    copies = [
+        pltpu.make_async_copy(ig_ref, ig_hbm, sem.at[0]),
+        pltpu.make_async_copy(wg_ref, wg_hbm, sem.at[1]),
+    ]
+    for copy in copies:
+        copy.start()
+    for copy in copies:
+        copy.wait()
+
+
 def body(input_field, grad_out, weight, filt, zonal_weight, widths, offsets, polar_rows):
     dma = pltpu.SemaphoreType.DMA
     hbm = pl.BlockSpec(memory_space=pltpu.HBM)
     vmem = pl.BlockSpec(memory_space=pltpu.VMEM)
-    smem = pl.BlockSpec(memory_space=pltpu.SMEM)
     groups, runs = len(GROUPS), len(RUNS)
-    return pl.pallas_call(
+    grads = pl.pallas_call(
         kernel,
         out_shape=(pltpu.VMEM((ROWS, LONS, C), BF16), pltpu.VMEM((72, C), F32)),
-        in_specs=[hbm, hbm, hbm, vmem, hbm, smem, smem, smem],
+        in_specs=[hbm] * 8,
         out_specs=(vmem, vmem),
         scratch_shapes=[
+            pltpu.VMEM((K, 3, ROWS, 2 * REACH + 1), BF16),
+            pltpu.SMEM((ROWS,), jnp.int32), pltpu.SMEM((ROWS,), jnp.int32), pltpu.SMEM((4,), jnp.int32),
             pltpu.VMEM((8, LONS + 2 * REACH, C), BF16),
+            pltpu.VMEM((2, LONS + 2 * REACH, C), BF16),
             pltpu.VMEM((ROWS, LONS, C), BF16),
             pltpu.VMEM((C, ROWS * LONS), BF16),
             pltpu.VMEM((K * C, C), BF16),
             pltpu.VMEM((K * C, C), BF16),
             pltpu.VMEM((CANDS, 128, 2 * REACH + 1), F32),
             pltpu.VMEM((8, 16, DEPTH), BF16),
-            pltpu.VMEM((2, 2, 16, DEPTH), BF16),
+            pltpu.VMEM((2, 16, DEPTH), BF16),
+            pltpu.VMEM((2, 16, DEPTH), BF16),
             pltpu.VMEM((32, DEPTH), F32),
+            pltpu.VMEM((32, 256), F32),
             pltpu.VMEM((ROWS, K * JB, DEPTH), BF16),
+            pltpu.VMEM((2, K * JB, 256), BF16),
+            pltpu.VMEM((8, K * JB, C), F32),
             pltpu.VMEM((ROWS * LONS, K * C), BF16),
+            pltpu.VMEM((K, C, C), F32),
             pltpu.VMEM((K, 3, ROWS, LONS), BF16),
             pltpu.VMEM((16, K * LONS), F32),
             pltpu.VMEM((2, 256, 128), F32),
@@ -622,6 +680,7 @@
             pltpu.VMEM((2, 32, LONS), BF16),
             pltpu.VMEM((ROWS, 32, LONS), BF16),
             pltpu.VMEM((32, C), F32),
+            pltpu.VMEM((64, C), BF16),
             pltpu.VMEM((C, 32), F32),
             pltpu.VMEM((8, C), F32),
             pltpu.VMEM((N_LON, 8, C), F32),
@@ -637,7 +696,7 @@
             pltpu.VMEM((2, N_Z, 16, 128), BF16),
             pltpu.VMEM((2, 16, 128), F32),
             pltpu.VMEM((2, 144, 128), F32),
-            dma((4,)), dma((8,)), dma((8,)), dma((2,)), dma((2,)), dma, dma, dma((2, N_LON)), dma,
+            dma((8,)), dma((8,)), dma((8,)), dma((2,)), dma((2,)), dma, dma, dma((2, N_LON)), dma,
             dma((groups,)), dma((groups,)), dma((runs, 4)), dma((runs,)), dma((runs, 4)), dma((runs,)),
             dma((K,)), dma((2,)), dma((2, 2, N_LON)), dma,
         ],
@@ -652,6 +711,17 @@
             jnp.transpose(zonal_weight, (0, 2, 1, 3)), widths, offsets, polar_rows,
         )
     ])
+    return tuple(pl.pallas_call(
+        store,
+        out_shape=(
+            jax.ShapeDtypeStruct((ROWS, LONS, C), BF16),
+            jax.ShapeDtypeStruct((72, C), F32),
+        ),
+        in_specs=[pl.BlockSpec(memory_space=pl.ANY)] * 2,
+        out_specs=(pl.BlockSpec(memory_space=pl.ANY),) * 2,
+        scratch_shapes=[dma((2,))],
+        name="store",
+    )(*[pltpu.with_memory_space_constraint(array, pltpu.VMEM) for array in grads]))
 
 
 def solution(mesh):

time: 50.5 us -> 43.8 us (0.87)
  Pallas kernels: 48.2 us -> 43 us
  local copies, waits for them, and re-layouts: 1.43 us -> 0 us
    pallas_call x1, Pallas kernels: 48.2 us -> 42.2 us  [body(): pl.pallas_call(kernel, out_shape=(pltpu.VMEM((ROWS, LONS, C), BF16), pltp...]
    unnamed x2 -> x0, local copies, waits for them, and re-layouts: 1.43 us -> none
    pallas_call x0 -> x1, Pallas kernels: none -> 0.82 us  [body(): pl.pallas_call(store, out_shape=(jax.ShapeDtypeStruct((ROWS, LONS, C), BF...]
where the time goes in v4:
time: 43.8 us; the launch traced here: 43.7 us
  Pallas kernels  43 us (98%)
  between operations  0.64 us (1%)
    pallas_call x1, Pallas kernels, body(): pl.pallas_call(kernel, out_shape=(pltpu.VMEM((ROWS, LONS, C), BF16), pltp...  42.2 us

profile of v4, /device:TPU:1, one launch (start us, length us, event | category | flops | bytes accessed | tf_op | source)
XLA Modules:
  0.0 43.7 jit_solution(18145864317976216708)
XLA Ops:
  0.6 42.2 %sphere_backward.1 = (bf16[4,256,256]{2,1,0:T(8,128)(2,1)S(1)}, f32[72,256]{1,0:T(8,128)S(1)}) custom-call(bf16[4,256,256]{2,1,0:T(8,128)(2,1)} %g_hbm.1, bf16[4,256,256]{2,1,0:T(8,128)(2,1)} %x_hbm.1, bf16[2304,256]{1,0:T(8,128)(2,1)} %w_hbm.1, bf16[9,3,4,33]{3,2,1,0:T(4,128)(2,1)} %bitcast.3, bf16[9,3,4,2048]{3,2,1,0:T(4,128)(2,1)} %bitcast.2, ...), custom_call_target="tpu_custom_call" | custom-call | tf_op jit(solution)/shard_map/sphere_backward/pallas_call | solution.py:651
  42.9 0.8 %store.1 = (bf16[4,256,256]{2,1,0:T(8,128)(2,1)}, f32[72,256]{1,0:T(8,128)}) custom-call(bf16[4,256,256]{2,1,0:T(8,128)(2,1)S(1)} %get-tuple-element.4.ig_ref, f32[72,256]{1,0:T(8,128)S(1)} %get-tuple-element.5.wg_ref), custom_call_target="tpu_custom_call" | custom-call | tf_op jit(solution)/shard_map/store/pallas_call | solution.py:714

commit v5 on v4

--- a/solution.py
+++ b/solution.py
@@ -23,9 +23,7 @@
 N_LAT = 32
 N_LON = 8
 N_Z = 8
-GROUPS = ((0, 4), (4, 7), (7, 9))
-RUNS = ((0, 2, "y"), (2, 4, "x"), (4, 6, "x"), (6, 7, "y"), (7, 8, "y"), (8, 9, "x"))
-GROUP_RUNS = ((0, 1), (2, 3), (4, 5))
+GROUPS = ((0, 2), (2, 5), (5, 9))
 FACTOR = 1.0 / math.sqrt(128 * 2048)
 
 
@@ -38,9 +36,9 @@
     ig_ref, wg_ref,
     filt_ref, width_ref, offset_ref, polar_ref,
     gx, gfar, xv, xt, wv, wt, lv, vown, vtwin, vfar, vf, vfh, tt, tth, facc, hh, wnear, zv, zs, yf, yown, yh, yy, ztf, zparts, zst, gs_own, gs_buf, gsel,
-    wown, wsnd, cx, s1, r1, s2, r2, s3, r3, s4, fin,
+    wown, wsnd, cx, s1, rplane, s3, r3, s4, fin,
     loc_sem, halo_send, halo_recv, vsend, vrecv, ysend, yrecv, gs_send, gs_sem,
-    cs_send, cs_recv, send1, recv1, send2, recv2, send3, recv3, fs_send, fs_recv,
+    cs_send, cs_recv, send_plane, recv_plane, send3, recv3, fs_send, fs_recv,
 ):
     lat = lax.axis_index("lat")
     lon = lax.axis_index("lon")
@@ -48,12 +46,12 @@
     twin = lat + 1 - 2 * core
     z, in_plane = lax.div(lat, 4), lax.rem(lat, 4)
     x_high, x_low, y = lax.div(in_plane, 2), lax.div(lon, 4), lax.rem(lon, 4)
-    place = {"x": 2 * x_high + x_low, "y": y}
+    x = 2 * x_high + x_low
 
     def lon_at(step):
         return lax.rem(lon + step, N_LON)
 
-    def remote(src, dst, send, recv, to_lat, to_lon, tag="rs"):
+    def remote(src, dst, send, recv, to_lat, to_lon):
         return pltpu.make_async_remote_copy(
             src_ref=src, dst_ref=dst, send_sem=send, recv_sem=recv,
             device_id={"lat": to_lat, "lon": to_lon}, device_id_type=MESH,
@@ -155,7 +153,6 @@
             src, dst, to_lat = gx.at[pl.ds(2 + far, 2), cols], gfar.at[:, to_cols], outer
         return remote(
             src, dst, halo_send.at[index], halo_recv.at[index], to_lat, lon_at(dlon % N_LON),
-            "big" if kind == "far" and dlon == 0 else "halo",
         )
 
     def arrived(buffer, semaphore):
@@ -174,10 +171,10 @@
             arrived(place_of, halo_recv.at[index])
 
     def v_twin():
-        return remote(vown.at[pl.ds(6 - 6 * core, 2)], vtwin, vsend.at[0], vrecv.at[0], twin, lon, "halo")
+        return remote(vown.at[pl.ds(6 - 6 * core, 2)], vtwin, vsend.at[0], vrecv.at[0], twin, lon)
 
     def v_far():
-        return remote(vown.at[pl.ds(6 * core, 2)], vfar, vsend.at[1], vrecv.at[1], outer, lon, "halo")
+        return remote(vown.at[pl.ds(6 * core, 2)], vfar, vsend.at[1], vrecv.at[1], outer, lon)
 
     for move in level:
         halo("level", *move).start()
@@ -200,11 +197,11 @@
 
     def gs_copy(dc, step):
         return remote(
-            gs_own, gs_buf.at[lon], gs_send.at[dc, step], gs_sem, twin if dc else lat, lon_at(step), "halo"
+            gs_own, gs_buf.at[lon], gs_send.at[dc, step], gs_sem, twin if dc else lat, lon_at(step)
         )
 
     def y_halo(first):
-        return remote(yown.at[pl.ds(first, 2)], yh, ysend, yrecv, twin, lon, "halo")
+        return remote(yown.at[pl.ds(first, 2)], yh, ysend, yrecv, twin, lon)
 
     @pl.when(jnp.logical_not(polar_dev))
     def _():
@@ -318,6 +315,10 @@
         vf[pl.ds(16 * a, 16), :] = vown[2 + far + a].astype(F32)
     band_rows(vf, DEPTH, lambda a: tt.at[far + a])
 
+    arrive("level", level)
+    arrive("twin", to_twin[1:])
+    spread_near((0, 3))
+    spread_far_own()
     for i2 in range(ROWS):
         yy[i2] = yown[2 + i2]
 
@@ -355,10 +356,6 @@
                 picked = picked + total[i:i + 1] * (mine == i).astype(F32)
             gsel[pl.ds(q, 1), :] = picked
 
-    arrive("level", level)
-    arrive("twin", to_twin[1:])
-    spread_near((0, 3))
-    spread_far_own()
     near_lons = pl.ds(pl.multiple_of(near * LONS, 2 * LONS), 2 * LONS)
     far_lons = pl.ds(pl.multiple_of(far * LONS, 2 * LONS), 2 * LONS)
     for k in range(K):
@@ -395,70 +392,48 @@
             wsnd[k] = jnp.where(core == 0, second, first).astype(BF16)
         twin_copy(group).start()
 
-    def along(axis, step):
-        to = lax.rem(place[axis] + step, 4)
-        if axis == "y":
-            return to, lat, lon + to - y
+    def along_x(step):
+        to = lax.rem(x + step, 4)
         return to, lat + 2 * (lax.div(to, 2) - x_high), lon + 4 * (lax.rem(to, 2) - x_low)
 
-    def first_piece(run, to):
-        k0, k1, axis = RUNS[run]
+    def plane_copy(group, dx, dy):
+        k0, k1 = GROUPS[group]
         at = pl.ds(k0, k1 - k0)
-        return s1.at[at, to] if axis == "y" else s1.at[at, :, to]
-
-    def first_copy(run, step):
-        k0, k1, axis = RUNS[run]
-        to, to_lat, to_lon = along(axis, step)
-        dst = r1.at[place[axis], pl.ds(k0, k1 - k0)]
-        return remote(first_piece(run, to), dst, send1.at[run, step], recv1.at[run], to_lat, to_lon, "r2")
-
-    def second_copy(run, step):
-        k0, k1, axis = RUNS[run]
-        axis = "x" if axis == "y" else "y"
-        to, to_lat, to_lon = along(axis, step)
-        at = pl.ds(k0, k1 - k0)
+        to_x, to_lat, to_lon = along_x(dx)
+        to_y = lax.rem(y + dy, 4)
+        slot = 4 * dx + dy
         return remote(
-            s2.at[at, to], r2.at[place[axis], at], send2.at[run, step], recv2.at[run], to_lat, to_lon, "r2"
+            s1.at[at, to_y, to_x], rplane.at[slot, at], send_plane.at[group, slot], recv_plane.at[group],
+            to_lat, to_lon + to_y - y,
         )
+
+    others = [(dx, dy) for dx in range(4) for dy in range(4) if dx or dy]
 
     def first(group):
         twin_copy(group).wait_recv()
         for k in range(*GROUPS[group]):
             s1[k] = (wown[k] + cx[k].astype(F32)).astype(BF16).reshape(4, 4, 16, 128)
-        for run in GROUP_RUNS[group]:
-            for step in range(1, 4):
-                first_copy(run, step).start()
-
-    def second(run):
-        k0, k1, axis = RUNS[run]
-        arrived(r1.at[pl.ds(0, 3), pl.ds(k0, k1 - k0)], recv1.at[run])
-        for k in range(k0, k1):
-            total = (s1[k, place[axis]] if axis == "y" else s1[k, :, place[axis]]).astype(F32)
-            for step in range(1, 4):
-                total = total + r1[lax.rem(place[axis] + step, 4), k].astype(F32)
-            s2[k] = total.astype(BF16)
-        for step in range(1, 4):
-            second_copy(run, step).start()
-
-    part = 4 * y + place["x"]
+        for dx, dy in others:
+            plane_copy(group, dx, dy).start()
+
+    part = 4 * y + x
 
     def granule(k):
         q = 16 * k + part
         to_z = lax.div(q, 18)
         b = lax.div(q - 18 * to_z, 16)
         copy = remote(
-            s3.at[k], r3.at[b, z], send3.at[k], recv3.at[b], 4 * to_z + in_plane, lon, "r3"
+            s3.at[k], r3.at[b, z], send3.at[k], recv3.at[b], 4 * to_z + in_plane, lon
         )
         return to_z, b, copy
 
-    def third(run):
-        k0, k1, axis = RUNS[run]
-        axis = "x" if axis == "y" else "y"
-        arrived(r2.at[pl.ds(0, 3), pl.ds(k0, k1 - k0)], recv2.at[run])
+    def second(group):
+        k0, k1 = GROUPS[group]
+        arrived(rplane.at[pl.ds(1, 15), pl.ds(k0, k1 - k0)], recv_plane.at[group])
         for k in range(k0, k1):
-            total = s2[k, place[axis]].astype(F32)
-            for step in range(1, 4):
-                total = total + r2[lax.rem(place[axis] + step, 4), k].astype(F32)
+            total = s1[k, y, x].astype(F32)
+            for dx, dy in others:
+                total = total + rplane[4 * dx + dy, k].astype(F32)
             s3[k] = total.astype(BF16)
         for k in range(k0, k1):
             to_z, b, copy = granule(k)
@@ -479,7 +454,7 @@
     def final_copy(b, to_high, e, dc, step):
         at = pl.ds(pl.multiple_of(16 * e, 16), 16)
         to_lat = 4 * z + 2 * to_high + (1 - core if dc else core)
-        return remote(s4.at[b], fin.at[core, at], fs_send.at[b, dc, step], fs_recv, to_lat, lon_at(step), "r4")
+        return remote(s4.at[b], fin.at[core, at], fs_send.at[b, dc, step], fs_recv, to_lat, lon_at(step))
 
     def needed(e, to_core):
         return ((to_core == 0) & (e <= 4)) | ((to_core == 1) & (e >= 4))
@@ -556,21 +531,12 @@
     mix(2)
     first(1)
     first(2)
+    prepare_pull()
+    pull(0)
     second(0)
     second(1)
-    prepare_pull()
-    pull(0)
+    pull(1)
     second(2)
-    second(3)
-    third(0)
-    third(1)
-    second(4)
-    second(5)
-    pull(1)
-    third(2)
-    third(3)
-    third(4)
-    third(5)
     spread_out()
     for move in level:
         halo("level", *move).wait_send()
@@ -601,10 +567,9 @@
 
     for group in range(len(GROUPS)):
         twin_copy(group).wait_send()
-    for run in range(len(RUNS)):
-        for step in range(1, 4):
-            first_copy(run, step).wait_send()
-            second_copy(run, step).wait_send()
+    for group in range(len(GROUPS)):
+        for dx, dy in others:
+            plane_copy(group, dx, dy).wait_send()
     for k in range(K):
         to_z, b, copy = granule(k)
 
@@ -647,7 +612,7 @@
     dma = pltpu.SemaphoreType.DMA
     hbm = pl.BlockSpec(memory_space=pltpu.HBM)
     vmem = pl.BlockSpec(memory_space=pltpu.VMEM)
-    groups, runs = len(GROUPS), len(RUNS)
+    groups = len(GROUPS)
     grads = pl.pallas_call(
         kernel,
         out_shape=(pltpu.VMEM((ROWS, LONS, C), BF16), pltpu.VMEM((72, C), F32)),
@@ -689,16 +654,13 @@
             pltpu.VMEM((K, C, 128), BF16),
             pltpu.VMEM((K, C, 128), BF16),
             pltpu.VMEM((K, 4, 4, 16, 128), BF16),
-            pltpu.VMEM((4, K, 4, 16, 128), BF16),
-            pltpu.VMEM((K, 4, 16, 128), BF16),
-            pltpu.VMEM((4, K, 16, 128), BF16),
+            pltpu.VMEM((16, K, 16, 128), BF16),
             pltpu.VMEM((K, 16, 128), BF16),
             pltpu.VMEM((2, N_Z, 16, 128), BF16),
             pltpu.VMEM((2, 16, 128), F32),
             pltpu.VMEM((2, 144, 128), F32),
             dma((8,)), dma((8,)), dma((8,)), dma((2,)), dma((2,)), dma, dma, dma((2, N_LON)), dma,
-            dma((groups,)), dma((groups,)), dma((runs, 4)), dma((runs,)), dma((runs, 4)), dma((runs,)),
-            dma((K,)), dma((2,)), dma((2, 2, N_LON)), dma,
+            dma((groups,)), dma((groups,)), dma((groups, 16)), dma((groups,)), dma((K,)), dma((2,)), dma((2, 2, N_LON)), dma,
         ],
         compiler_params=pltpu.CompilerParams(
             collective_id=0, has_side_effects=True, vmem_limit_bytes=48 * 1024 * 1024

time: 43.8 us -> 41.9 us (0.957); the launches traced: 43.7 us -> 41.3 us
  Pallas kernels: 43 us -> 40.6 us
    pallas_call x1, Pallas kernels: 42.2 us -> 39.8 us  [body(): pl.pallas_call(kernel, out_shape=(pltpu.VMEM((ROWS, LONS, C), BF16), pltp...]
where the time goes in v5:
time: 41.9 us; the launch traced here: 41.3 us
  Pallas kernels  40.6 us (97%)
  between operations  0.64 us (2%)
    pallas_call x1, Pallas kernels, body(): pl.pallas_call(kernel, out_shape=(pltpu.VMEM((ROWS, LONS, C), BF16), pltp...  39.8 us

profile of v5, /device:TPU:1, one launch (start us, length us, event | category | flops | bytes accessed | tf_op | source)
XLA Modules:
  0.0 41.3 jit_solution(4311952495173580717)
XLA Ops:
  0.6 39.8 %sphere_backward.1 = (bf16[4,256,256]{2,1,0:T(8,128)(2,1)S(1)}, f32[72,256]{1,0:T(8,128)S(1)}) custom-call(bf16[4,256,256]{2,1,0:T(8,128)(2,1)} %g_hbm.1, bf16[4,256,256]{2,1,0:T(8,128)(2,1)} %x_hbm.1, bf16[2304,256]{1,0:T(8,128)(2,1)} %w_hbm.1, bf16[9,3,4,33]{3,2,1,0:T(4,128)(2,1)} %bitcast.3, bf16[9,3,4,2048]{3,2,1,0:T(4,128)(2,1)} %bitcast.2, ...), custom_call_target="tpu_custom_call" | custom-call | tf_op jit(solution)/shard_map/sphere_backward/pallas_call | solution.py:616
  40.4 0.8 %store.1 = (bf16[4,256,256]{2,1,0:T(8,128)(2,1)}, f32[72,256]{1,0:T(8,128)}) custom-call(bf16[4,256,256]{2,1,0:T(8,128)(2,1)S(1)} %get-tuple-element.4.ig_ref, f32[72,256]{1,0:T(8,128)S(1)} %get-tuple-element.5.wg_ref), custom_call_target="tpu_custom_call" | custom-call | tf_op jit(solution)/shard_map/store/pallas_call | solution.py:676

commit v6 on v5

--- a/solution.py
+++ b/solution.py
@@ -407,7 +407,10 @@
             to_lat, to_lon + to_y - y,
         )
 
-    others = [(dx, dy) for dx in range(4) for dy in range(4) if dx or dy]
+    others = sorted(
+        [(dx, dy) for dx in range(4) for dy in range(4) if dx or dy],
+        key=lambda move: -min(move[0], 4 - move[0]) - min(move[1], 4 - move[1]),
+    )
 
     def first(group):
         twin_copy(group).wait_recv()

time: 41.9 us -> 41.2 us (0.983)
  Pallas kernels: 40.6 us -> 40.1 us
    pallas_call x1, Pallas kernels: 39.8 us -> 39.3 us  [body(): pl.pallas_call(kernel, out_shape=(pltpu.VMEM((ROWS, LONS, C), BF16), pltp...]
where the time goes in v6:
time: 41.2 us; the launch traced here: 40.7 us
  Pallas kernels  40.1 us (97%)
  between operations  0.64 us (2%)
    pallas_call x1, Pallas kernels, body(): pl.pallas_call(kernel, out_shape=(pltpu.VMEM((ROWS, LONS, C), BF16), pltp...  39.3 us
    pallas_call x1, Pallas kernels, body(): pl.pallas_call(store, out_shape=(jax.ShapeDtypeStruct((ROWS, LONS, C), BF...  0.82 us

profile of v6, /device:TPU:1, one launch (start us, length us, event | category | flops | bytes accessed | tf_op | source)
XLA Modules:
  0.0 40.7 jit_solution(9295673492013358322)
XLA Ops:
  0.6 39.3 %sphere_backward.1 = (bf16[4,256,256]{2,1,0:T(8,128)(2,1)S(1)}, f32[72,256]{1,0:T(8,128)S(1)}) custom-call(bf16[4,256,256]{2,1,0:T(8,128)(2,1)} %g_hbm.1, bf16[4,256,256]{2,1,0:T(8,128)(2,1)} %x_hbm.1, bf16[2304,256]{1,0:T(8,128)(2,1)} %w_hbm.1, bf16[9,3,4,33]{3,2,1,0:T(4,128)(2,1)} %bitcast.3, bf16[9,3,4,2048]{3,2,1,0:T(4,128)(2,1)} %bitcast.2, ...), custom_call_target="tpu_custom_call" | custom-call | tf_op jit(solution)/shard_map/sphere_backward/pallas_call | solution.py:619
  39.9 0.8 %store.1 = (bf16[4,256,256]{2,1,0:T(8,128)(2,1)}, f32[72,256]{1,0:T(8,128)}) custom-call(bf16[4,256,256]{2,1,0:T(8,128)(2,1)S(1)} %get-tuple-element.4.ig_ref, f32[72,256]{1,0:T(8,128)S(1)} %get-tuple-element.5.wg_ref), custom_call_target="tpu_custom_call" | custom-call | tf_op jit(solution)/shard_map/store/pallas_call | solution.py:679

commit v7 on v6

--- a/solution.py
+++ b/solution.py
@@ -23,7 +23,7 @@
 N_LAT = 32
 N_LON = 8
 N_Z = 8
-GROUPS = ((0, 2), (2, 5), (5, 9))
+GROUPS = ((0, 2), (2, 4), (4, 6), (6, 9))
 FACTOR = 1.0 / math.sqrt(128 * 2048)
 
 
@@ -533,13 +533,17 @@
     spread_far(*GROUPS[2])
     mix(2)
     first(1)
+    spread_far(*GROUPS[3])
+    mix(3)
     first(2)
+    first(3)
     prepare_pull()
     pull(0)
     second(0)
     second(1)
     pull(1)
     second(2)
+    second(3)
     spread_out()
     for move in level:
         halo("level", *move).wait_send()

time: 41.2 us -> 41.3 us (level)
  no operation moved by 1% of the time
where the time goes in v7:
time: 41.3 us; the launch traced here: 40.8 us
  Pallas kernels  40.2 us (97%)
  between operations  0.64 us (2%)
    pallas_call x1, Pallas kernels, body(): pl.pallas_call(kernel, out_shape=(pltpu.VMEM((ROWS, LONS, C), BF16), pltp...  39.3 us

profile of v7, /device:TPU:1, one launch (start us, length us, event | category | flops | bytes accessed | tf_op | source)
XLA Modules:
  0.0 40.8 jit_solution(885956747771019189)
XLA Ops:
  0.6 39.3 %sphere_backward.1 = (bf16[4,256,256]{2,1,0:T(8,128)(2,1)S(1)}, f32[72,256]{1,0:T(8,128)S(1)}) custom-call(bf16[4,256,256]{2,1,0:T(8,128)(2,1)} %g_hbm.1, bf16[4,256,256]{2,1,0:T(8,128)(2,1)} %x_hbm.1, bf16[2304,256]{1,0:T(8,128)(2,1)} %w_hbm.1, bf16[9,3,4,33]{3,2,1,0:T(4,128)(2,1)} %bitcast.3, bf16[9,3,4,2048]{3,2,1,0:T(4,128)(2,1)} %bitcast.2, ...), custom_call_target="tpu_custom_call" | custom-call | tf_op jit(solution)/shard_map/sphere_backward/pallas_call | solution.py:623
  40.0 0.8 %store.1 = (bf16[4,256,256]{2,1,0:T(8,128)(2,1)}, f32[72,256]{1,0:T(8,128)}) custom-call(bf16[4,256,256]{2,1,0:T(8,128)(2,1)S(1)} %get-tuple-element.4.ig_ref, f32[72,256]{1,0:T(8,128)S(1)} %get-tuple-element.5.wg_ref), custom_call_target="tpu_custom_call" | custom-call | tf_op jit(solution)/shard_map/store/pallas_call | solution.py:683
